TPU v7x, 32 devices: a whole 2x2x4 slice. The times are simulated.
32 devices in a mesh: rep: 8 (over z, y), fsdp: 4 (over x, core).
Axes of the slice: x: 2, y: 2, z: 4, core: 2. Of those that a mesh axis runs over, the one named last changes fastest.
Arguments:
- tokens: bfloat16 [8192, 960], P(('rep', 'fsdp')), may hold values from -6 to 6
- cotangent: bfloat16 [8192, 960], P(('rep', 'fsdp')), may hold values from -6 to 6
- lengths: int32 [8, 8], P('rep'), may hold values from 0 to 1024, as said below
- norm1_gain: bfloat16 [960], P('fsdp'), may hold values from 0.5 to 1.5
- w_query: bfloat16 [960, 960], P('fsdp'), may hold values from -0.1875 to 0.1875
- w_key: bfloat16 [960, 320], P('fsdp'), may hold values from -0.1875 to 0.1875
- w_value: bfloat16 [960, 320], P('fsdp'), may hold values from -0.1875 to 0.1875
- w_out: bfloat16 [960, 960], P('fsdp'), may hold values from -0.75 to 0.75
- norm2_gain: bfloat16 [960], P('fsdp'), may hold values from 0.5 to 1.5
- w_gate: bfloat16 [960, 2560], P('fsdp'), may hold values from -0.1875 to 0.1875
- w_up: bfloat16 [960, 2560], P('fsdp'), may hold values from -0.1875 to 0.1875
- w_down: bfloat16 [2560, 960], P('fsdp'), may hold values from -0.125 to 0.125
Outputs:
- mixed: bfloat16 [8192, 960], P(('rep', 'fsdp'))
- tokens_grad: bfloat16 [8192, 960], P(('rep', 'fsdp'))
- norm1_grad: float32 [960], P('fsdp')
- query_grad: float32 [960, 960], P('fsdp')
- key_grad: float32 [960, 320], P('fsdp')
- value_grad: float32 [960, 320], P('fsdp')
- out_grad: float32 [960, 960], P('fsdp')
- norm2_grad: float32 [960], P('fsdp')
- gate_grad: float32 [960, 2560], P('fsdp')
- up_grad: float32 [960, 2560], P('fsdp')
- down_grad: float32 [2560, 960], P('fsdp')
Inputs may be any that keep to these rules, and one draw needn't show every extreme that they name: Row g lists the lengths of the documents packed in order into the 1024 tokens of group g; each row sums to 1024; a length 0 is an empty slot.
All inputs are finite; a program needn't handle non-finite values.
Results may differ from a plain program's by a relative error of at most 0.02.
Values may be sent and summed in bfloat16 or wider, within the bound.
A program may use at most 192 MiB of HBM per device.

v0:
```python
import jax
import jax.numpy as jnp
from jax import lax
from jax.sharding import PartitionSpec as P

HEAD_DIM = 64


EPS = 1e-05
THETA = 100000.0


def doc_layout(lens, count):
    ends = jnp.cumsum(lens)
    starts = ends - lens
    place = jnp.arange(count, dtype=jnp.int32)
    segment = jnp.sum((place[:, None] >= ends[None, :]).astype(jnp.int32), axis=1)
    owner = segment[:, None] == jnp.arange(lens.shape[0], dtype=jnp.int32)[None, :]
    offset = jnp.sum(jnp.where(owner, starts[None, :], 0), axis=1)
    return (segment, place - offset)


def rotate(heads, position, sign):
    half = heads.shape[-1] // 2
    freq = THETA ** (-jnp.arange(half, dtype=jnp.float32) * 2.0 / heads.shape[-1])
    angle = position.astype(jnp.float32)[:, None] * freq[None, :]
    cosine = jnp.cos(angle)[:, None, :]
    sine = sign * jnp.sin(angle)[:, None, :]
    first = heads[..., :half]
    second = heads[..., half:]
    return jnp.concatenate(
        [first * cosine - second * sine, second * cosine + first * sine], axis=-1
    )


def matmul(left, right):
    return jnp.dot(left, right, preferred_element_type=jnp.float32)


def left_inner(left, right):
    return lax.dot_general(
        left, right, (((0,), (0,)), ((), ())), preferred_element_type=jnp.float32
    )


def right_inner(left, right):
    return lax.dot_general(
        left, right, (((1,), (1,)), ((), ())), preferred_element_type=jnp.float32
    )


def norm_back(values, inverse, gain, upstream):
    scaled = gain * upstream
    gain_part = jnp.sum(upstream * values * inverse, axis=0)
    input_part = inverse * scaled - values * inverse**3 * jnp.mean(
        scaled * values, axis=-1, keepdims=True
    )
    return (gain_part, input_part)


def body(
    tokens,
    cotangent,
    lengths,
    norm1_gain,
    w_query,
    w_key,
    w_value,
    w_out,
    norm2_gain,
    w_gate,
    w_up,
    w_down,
):
    shards = (norm1_gain, w_query, w_key, w_value, w_out, norm2_gain, w_gate, w_up, w_down)
    gathered = (
        lax.all_gather(norm1_gain, "fsdp", axis=0, tiled=True),
        lax.all_gather(w_query, "fsdp", axis=0, tiled=True),
        lax.all_gather(w_key, "fsdp", axis=0, tiled=True),
        lax.all_gather(w_value, "fsdp", axis=0, tiled=True),
        lax.all_gather(w_out, "fsdp", axis=0, tiled=True),
        lax.all_gather(norm2_gain, "fsdp", axis=0, tiled=True),
        lax.all_gather(w_gate, "fsdp", axis=0, tiled=True),
        lax.all_gather(w_up, "fsdp", axis=0, tiled=True),
        lax.all_gather(w_down, "fsdp", axis=0, tiled=True),
    )
    (
        gain_one,
        query_weight,
        key_weight,
        value_weight,
        out_weight,
        gain_two,
        gate_weight,
        up_weight,
        down_weight,
    ) = gathered
    count = tokens.shape[0]
    ways = lax.axis_size("fsdp")
    total = count * ways
    head_dim = HEAD_DIM
    scale = head_dim ** (-0.5)
    segment_all, position_all = doc_layout(lengths[0], total)
    first_row = lax.axis_index("fsdp") * count
    segment_mine = lax.dynamic_slice_in_dim(segment_all, first_row, count)
    position_mine = lax.dynamic_slice_in_dim(position_all, first_row, count)
    place_mine = first_row + jnp.arange(count, dtype=jnp.int32)
    inputs = tokens.astype(jnp.float32)
    inverse_one = lax.rsqrt(jnp.mean(inputs * inputs, axis=-1, keepdims=True) + EPS)
    gain_one_f = gain_one.astype(jnp.float32)
    normed_one = (inputs * inverse_one * gain_one_f).astype(jnp.bfloat16)
    query = rotate(
        matmul(normed_one, query_weight).reshape(count, -1, head_dim), position_mine, 1.0
    ).astype(jnp.bfloat16)
    key_local = rotate(
        matmul(normed_one, key_weight).reshape(count, -1, head_dim), position_mine, 1.0
    ).astype(jnp.bfloat16)
    value_local = matmul(normed_one, value_weight).astype(jnp.bfloat16)
    all_keys, all_values = (
        lax.all_gather(key_local.reshape(count, -1), "fsdp", axis=0, tiled=True),
        lax.all_gather(value_local, "fsdp", axis=0, tiled=True),
    )
    groups = all_keys.shape[1] // head_dim
    share = query.shape[1] // groups
    grouped = query.reshape(count, groups, share, head_dim)
    key_block = min(512, total)
    nblocks = total // key_block
    key_blocks = all_keys.reshape(nblocks, key_block, groups, head_dim)
    value_blocks = all_values.reshape(nblocks, key_block, groups, head_dim)
    segment_blocks = segment_all.reshape(nblocks, key_block)
    place_blocks = jnp.arange(total, dtype=jnp.int32).reshape(nblocks, key_block)

    def scores_for(keys_here, segment_here, place_here):
        allowed = (place_here[None, :] <= place_mine[:, None]) & (
            segment_here[None, :] == segment_mine[:, None]
        )
        raw = (
            jnp.einsum("bgrd,kgd->grbk", grouped, keys_here, preferred_element_type=jnp.float32)
            * scale
        )
        return (jnp.where(allowed[None, None], raw, -1e30), allowed[None, None])

    def gather_stats(carry, item):
        top, mass = carry
        keys_here, values_here, segment_here, place_here = item
        raw, allowed = scores_for(keys_here, segment_here, place_here)
        new_top = jnp.maximum(top, jnp.max(raw, axis=-1, keepdims=True))
        expo = jnp.where(allowed, jnp.exp(raw - new_top), 0.0)
        mass = mass * jnp.exp(top - new_top) + jnp.sum(expo, axis=-1, keepdims=True)
        return ((new_top, mass), None)

    stack = (key_blocks, value_blocks, segment_blocks, place_blocks)
    start_top = jnp.full((groups, share, count, 1), -1e30, jnp.float32)
    start_mass = jnp.zeros((groups, share, count, 1), jnp.float32)
    (top_all, mass_all), unused = lax.scan(gather_stats, (start_top, start_mass), stack)
    log_total = top_all + jnp.log(mass_all)

    def probs_for(item):
        keys_here, values_here, segment_here, place_here = item
        raw, allowed = scores_for(keys_here, segment_here, place_here)
        return jnp.where(allowed, jnp.exp(raw - log_total), 0.0)

    def mix_values(carry, item):
        probs = probs_for(item).astype(jnp.bfloat16)
        return (
            carry
            + jnp.einsum("grbk,kgd->bgrd", probs, item[1], preferred_element_type=jnp.float32),
            None,
        )

    attended, unused = lax.scan(
        mix_values, jnp.zeros((count, groups, share, head_dim), jnp.float32), stack
    )
    attended_flat = attended.reshape(count, -1)
    attended_low = attended_flat.astype(jnp.bfloat16)
    resid = inputs + matmul(attended_low, out_weight)
    inverse_two = lax.rsqrt(jnp.mean(resid * resid, axis=-1, keepdims=True) + EPS)
    gain_two_f = gain_two.astype(jnp.float32)
    normed_two = (resid * inverse_two * gain_two_f).astype(jnp.bfloat16)
    gate = matmul(normed_two, gate_weight)
    up_proj = matmul(normed_two, up_weight)
    sigma = jax.nn.sigmoid(gate)
    activated = gate * sigma
    hidden = (activated * up_proj).astype(jnp.bfloat16)
    mixed = (resid + matmul(hidden, down_weight)).astype(jnp.bfloat16)
    again = (
        lax.all_gather(norm1_gain, "fsdp", axis=0, tiled=True),
        lax.all_gather(w_query, "fsdp", axis=0, tiled=True),
        lax.all_gather(w_key, "fsdp", axis=0, tiled=True),
        lax.all_gather(w_value, "fsdp", axis=0, tiled=True),
        lax.all_gather(w_out, "fsdp", axis=0, tiled=True),
        lax.all_gather(norm2_gain, "fsdp", axis=0, tiled=True),
        lax.all_gather(w_gate, "fsdp", axis=0, tiled=True),
        lax.all_gather(w_up, "fsdp", axis=0, tiled=True),
        lax.all_gather(w_down, "fsdp", axis=0, tiled=True),
    )
    (
        gain_one,
        query_weight,
        key_weight,
        value_weight,
        out_weight,
        gain_two,
        gate_weight,
        up_weight,
        down_weight,
    ) = again
    gain_one_f = gain_one.astype(jnp.float32)
    gain_two_f = gain_two.astype(jnp.float32)
    upstream = cotangent.astype(jnp.float32)
    down_grad = left_inner(hidden, cotangent)
    hidden_back = right_inner(cotangent, down_weight)
    gate_back = (hidden_back * up_proj * sigma * (1.0 + gate * (1.0 - sigma))).astype(jnp.bfloat16)
    up_back = (hidden_back * activated).astype(jnp.bfloat16)
    gate_grad = left_inner(normed_two, gate_back)
    up_grad = left_inner(normed_two, up_back)
    normed_two_back = right_inner(gate_back, gate_weight) + right_inner(up_back, up_weight)
    norm2_grad, resid_part = norm_back(resid, inverse_two, gain_two_f, normed_two_back)
    resid_back = upstream + resid_part
    branch_back = resid_back.astype(jnp.bfloat16)
    out_grad = left_inner(attended_low, branch_back)
    attended_back = right_inner(branch_back, out_weight).astype(jnp.bfloat16)
    back_heads = attended_back.reshape(count, groups, share, head_dim)
    delta = jnp.sum(back_heads.astype(jnp.float32) * attended, axis=-1).transpose(1, 2, 0)[
        ..., None
    ]

    def attend_back(carry, item):
        probs = probs_for(item)
        keys_here = item[0]
        values_here = item[1]
        values_back = jnp.einsum(
            "grbk,bgrd->kgd",
            probs.astype(jnp.bfloat16),
            back_heads,
            preferred_element_type=jnp.float32,
        )
        prob_back = jnp.einsum(
            "bgrd,kgd->grbk", back_heads, values_here, preferred_element_type=jnp.float32
        )
        score_back = (probs * (prob_back - delta)).astype(jnp.bfloat16)
        carry = carry + jnp.einsum(
            "grbk,kgd->bgrd", score_back, keys_here, preferred_element_type=jnp.float32
        )
        keys_back = (
            jnp.einsum("grbk,bgrd->kgd", score_back, grouped, preferred_element_type=jnp.float32)
            * scale
        )
        return (carry, (keys_back, values_back))

    query_acc, kv_back = lax.scan(
        attend_back, jnp.zeros((count, groups, share, head_dim), jnp.float32), stack
    )
    keys_back_all = kv_back[0].reshape(total, -1)
    values_back_all = kv_back[1].reshape(total, -1)
    keys_back, values_back = (
        lax.psum_scatter(
            keys_back_all.astype(jnp.bfloat16), "fsdp", scatter_dimension=0, tiled=True
        ).astype(jnp.float32),
        lax.psum_scatter(
            values_back_all.astype(jnp.bfloat16), "fsdp", scatter_dimension=0, tiled=True
        ).astype(jnp.float32),
    )
    key_pre = (
        rotate(keys_back.reshape(count, -1, head_dim), position_mine, -1.0)
        .reshape(count, -1)
        .astype(jnp.bfloat16)
    )
    value_pre = values_back.astype(jnp.bfloat16)
    query_pre = (
        rotate((query_acc * scale).reshape(count, -1, head_dim), position_mine, -1.0)
        .reshape(count, -1)
        .astype(jnp.bfloat16)
    )
    query_grad = left_inner(normed_one, query_pre)
    key_grad = left_inner(normed_one, key_pre)
    value_grad = left_inner(normed_one, value_pre)
    normed_one_back = (
        right_inner(query_pre, query_weight)
        + right_inner(key_pre, key_weight)
        + right_inner(value_pre, value_weight)
    )
    norm1_grad, input_part = norm_back(inputs, inverse_one, gain_one_f, normed_one_back)
    tokens_grad = (resid_back + input_part).astype(jnp.bfloat16)
    grads = (
        norm1_grad,
        query_grad,
        key_grad,
        value_grad,
        out_grad,
        norm2_grad,
        gate_grad,
        up_grad,
        down_grad,
    )
    packed = jnp.concatenate([grad.reshape(ways, -1) for grad in grads], axis=1)
    width = packed.shape[1]
    replicas = lax.axis_size("rep")
    padding = -width % replicas
    piece_len = (width + padding) // replicas
    shard_sum = lax.psum_scatter(
        packed.astype(jnp.bfloat16), "fsdp", scatter_dimension=0, tiled=True
    ).astype(jnp.float32)
    spread = jnp.pad(shard_sum.reshape(-1), (0, padding)).reshape(replicas, piece_len)
    piece = lax.psum_scatter(spread, "rep", scatter_dimension=0, tiled=True)
    whole = lax.all_gather(piece.astype(jnp.bfloat16), "rep", axis=0, tiled=True).astype(
        piece.dtype
    )
    summed = whole.reshape(-1)[:width]
    results = []
    offset = 0
    for shard in shards:
        size_here = shard.size
        results.append(summed[offset : offset + size_here].reshape(shard.shape))
        offset = offset + size_here
    return (
        mixed,
        tokens_grad,
        results[0],
        results[1],
        results[2],
        results[3],
        results[4],
        results[5],
        results[6],
        results[7],
        results[8],
    )


def solution(mesh):
    return jax.shard_map(
        body,
        mesh=mesh,
        in_specs=(
            P(("rep", "fsdp"), None),
            P(("rep", "fsdp"), None),
            P("rep", None),
            P("fsdp"),
            P("fsdp", None),
            P("fsdp", None),
            P("fsdp", None),
            P("fsdp", None),
            P("fsdp"),
            P("fsdp", None),
            P("fsdp", None),
            P("fsdp", None),
        ),
        out_specs=(
            P(("rep", "fsdp"), None),
            P(("rep", "fsdp"), None),
            P("fsdp"),
            P("fsdp", None),
            P("fsdp", None),
            P("fsdp", None),
            P("fsdp", None),
            P("fsdp"),
            P("fsdp", None),
            P("fsdp", None),
            P("fsdp", None),
        ),
        check_vma=False,
    )
```

profile of v0, /device:TPU:0, one launch (start us, length us, event | category | flops | bytes accessed | tf_op | source)
XLA Modules:
  0.0 1647.7 jit_solution(11515797729400041167)
XLA Ops:
  10.8 9.5 all-gather
  23.3 7.2 all-reduce.4
  31.7 7.4 all_gather.47
  40.8 10.8 all-gather.1
  54.2 8.7 all_gather.49
  66.3 20.8 %while.39 = (s32[]{:T(128)}, f32[5,3,256,1]{2,1,0,3:T(4,128)S(1)}, f32[5,3,256,1]{2,1,0,3:T(4,128)S(1)}, s32[2,512]{1,0:T(2,128)S(1)}, s32[2,512]{1,0:T(2,128)S(...) while((s32[]{:T(128)}, f32[5,3,256,1]{2,1,0,3:T(4,128)S(1)}, ...), condition=%wide.region_7.8_spmd.clone, body=%wide.region_4.7_spmd.clone.sunk | while | flops 267799552 | bytes 17156236 | solution.py:155
  87.1 10.3 while.40
  108.0 33.0 %all-gather.16.cloned.1.call-done = bf16[960,2560]{1,0:T(8,128)(2,1)} async-done(((bf16[240,2560]{1,0:T(8,128)(2,1)}), bf16[960,2560]{1,0:T(8,128)(2,1)}) %all-gather.16.cloned.1.call-update) | async-done | bytes 4915216 | tf_op jit(solution)/shard_map/all_gather | solution.py:84
  141.0 5.5 fusion.100
  146.5 34.5 %all-gather.18.cloned.1.call-done = bf16[2560,960]{0,1:T(8,128)(2,1)} async-done(((bf16[640,960]{0,1:T(8,128)(2,1)}), bf16[2560,960]{0,1:T(8,128)(2,1)}) %all-gather.18.cloned.1.call-update) | async-done | bytes 4915216 | tf_op jit(solution)/shard_map/all_gather | solution.py:85
  181.0 7.8 multiply_convert_fusion
  199.3 29.3 %while.41 = (s32[]{:T(128)}, f32[256,5,3,64]{0,3,2,1:T(8,128)S(1)}, bf16[2,512,5,64]{1,3,2,0:T(8,128)(2,1)}, bf16[2,512,5,64]{1,3,2,0:T(8,128)(2,1)}, bf16[2,512...) while((s32[]{:T(128)}, f32[256,5,3,64]{0,3,2,1:T(8,128)S(1)}, ...), condition=%wide.region_14.15_spmd.clone, body=%wide.region_13.14_spmd.clone.sunk | while | flops 1282932992 | bytes 127277416 | solution.py:251
  262.6 8.5 reshape.466
  271.1 8.6 reshape.467
  279.7 8.1 copy.83
  287.8 10.5 reshape.527
  298.4 6.4 reshape.468
  324.9 18.6 %dynamic-update-slice.3 = bf16[4,2458080]{1,0:T(4,128)(2,1)} dynamic-update-slice(bf16[4,2458080]{1,0:T(4,128)(2,1)} %dynamic-update-slice.2, bf16[4,230400]{1,0:T(4,128)(2,1)} %reshape.461, s32[]{} %constant.118, s32[]{} %constant.119) | dynamic-update-slice | bytes 3686404
  343.5 7.1 dynamic-update-slice.4
  350.6 6.8 dynamic-update-slice.5
  357.5 17.7 %dynamic-update-slice.6 = bf16[4,2458080]{1,0:T(4,128)(2,1)} dynamic-update-slice(bf16[4,2458080]{1,0:T(4,128)(2,1)} %dynamic-update-slice.5, bf16[4,230400]{1,0:T(4,128)(2,1)S(1)} %reshape.464, s32[]{} %constant.118, s32[]{} %constant.122) | dynamic-update-slice | bytes 3686404
  376.7 47.2 %dynamic-update-slice.8 = bf16[4,2458080]{1,0:T(4,128)(2,1)} dynamic-update-slice(bf16[4,2458080]{1,0:T(4,128)(2,1)} %dynamic-update-slice.7, bf16[4,614400]{1,0:T(4,128)(2,1)} %reshape.466, s32[]{} %constant.118, s32[]{} %constant.124) | dynamic-update-slice | bytes 9830404
  423.8 47.2 %dynamic-update-slice.9 = bf16[4,2458080]{1,0:T(4,128)(2,1)} dynamic-update-slice(bf16[4,2458080]{1,0:T(4,128)(2,1)} %dynamic-update-slice.8, bf16[4,614400]{1,0:T(4,128)(2,1)} %reshape.467, s32[]{} %constant.118, s32[]{} %constant.125) | dynamic-update-slice | bytes 9830404
  471.0 47.0 %dynamic-update-slice.10 = bf16[4,2458080]{1,0:T(4,128)(2,1)} dynamic-update-slice(bf16[4,2458080]{1,0:T(4,128)(2,1)} %dynamic-update-slice.9, bf16[4,614400]{1,0:T(4,128)(2,1)} %reshape.468, s32[]{} %constant.118, s32[]{} %constant.126) | dynamic-update-slice | bytes 9830404 | tf_op jit(solution)/shard_map/concatenate | solution.py:296
  519.2 334.4 %all-reduce.8.cloned.1.call-done = bf16[4,2458080]{1,0:T(4,128)(2,1)} async-done(((bf16[4,2458080]{1,0:T(4,128)(2,1)}), bf16[4,2458080]{1,0:T(4,128)(2,1)}) %all-reduce.8.cloned.1.call-update) | async-done | bytes 19664656
  853.6 107.9 %fusion.69 = f32[2458080]{0:T(1024)} fusion(bf16[4,2458080]{1,0:T(4,128)(2,1)} %all-reduce.8.cloned.1.call-done, u32[]{:T(128)} %bitcast.65), kind=kLoop, calls=%fused_computation.76 | loop fusion | flops 2458080 | bytes 14748484 | tf_op jit(solution)/shard_map/reshape | solution.py:304
  961.5 12.7 reshape.483
  974.2 384.0 %all-reduce.9 = bf16[8,307260]{1,0:T(8,128)(2,1)} all-reduce(f32[8,307260]{1,0:T(8,128)} %reshape.483), channel_id=5, replica_groups=mesh['rep'=8,'fsdp'=4] {'rep'}, use_global_device_ids=true, to_apply=%region_21.22.clone | all-reduce | flops 2458080 | bytes 14748480
  1370.0 134.1 %all-gather.20.cloned.1.call-done = bf16[8,1,307260]{2,1,0:T(2,128)(2,1)} async-done(((bf16[1,1,307260]{2,1,0:T(2,128)(2,1)}), bf16[8,1,307260]{2,1,0:T(2,128)(2,1)}) %all-gather.20.cloned.1.call-update) | async-done | bytes 4916176 | tf_op jit(solution)/shard_map/all_gather | solution.py:306
  1504.1 89.5 %convert_reduce_fusion = f32[8,307260]{1,0:T(8,128)} fusion(bf16[8,1,307260]{2,1,0:T(2,128)(2,1)} %all-gather.20.cloned.1.call-done), kind=kLoop, calls=%fused_computation.74 | loop fusion | flops 2458080 | bytes 14748480 | tf_op jit(solution)/shard_map/reshape | solution.py:309
  1593.6 12.7 reshape.485
  1612.6 7.4 fusion.94
  (276 shorter events, 190.3 us)
Async XLA Ops:
  7.2 14.2 copy-start.41
  7.2 15.6 copy-start.42
  7.2 15.8 copy-start.43
  7.2 23.3 %copy-start.5 = (bf16[256,960]{0,1:T(8,128)(2,1)S(1)}, bf16[256,960]{0,1:T(8,128)(2,1)}, u32[]{:S(2)}) copy-start(bf16[256,960]{0,1:T(8,128)(2,1)} %param.18) | copy-start | bytes 1474564
  7.2 56.2 %all-gather.10.cloned.1.call-start = ((), (), s32[]{:S(2)}) async-start(), calls=%async_computation.2 | async-start | bytes 2457600 | tf_op jit(solution)/shard_map/all_gather | solution.py:78
  8.0 90.8 %all-gather.12.cloned.1.call-start = ((), (), s32[]{:S(2)}) async-start(), calls=%async_computation.3 | async-start | bytes 2457600 | tf_op jit(solution)/shard_map/all_gather | solution.py:81
  8.7 93.9 %all-gather.14.cloned.1.call-start = ((), (), s32[]{:S(2)}) async-start(), calls=%async_computation.4 | async-start | bytes 6144000 | tf_op jit(solution)/shard_map/all_gather | solution.py:83
  9.4 131.6 %all-gather.16.cloned.1.call-start = ((), (), s32[]{:S(2)}) async-start(), calls=%async_computation.5 | async-start | bytes 6144000 | tf_op jit(solution)/shard_map/all_gather | solution.py:84
  10.0 171.0 %all-gather.18.cloned.1.call-start = ((), (), s32[]{:S(2)}) async-start(), calls=%async_computation.6 | async-start | bytes 6144000 | tf_op jit(solution)/shard_map/all_gather | solution.py:85
  10.6 29.8 %copy-start.44 = (s32[1,8]{1,0:T(1,128)S(1)}, s32[1,8]{1,0:T(1,128)}, u32[]{:S(2)}) copy-start(s32[1,8]{1,0:T(1,128)} %param.20) | copy-start | bytes 100
  10.6 30.2 %copy-start.35 = (bf16[240,320]{0,1:T(8,128)(2,1)S(1)}, bf16[240,320]{0,1:T(8,128)(2,1)}, u32[]{:S(2)}) copy-start(bf16[240,320]{0,1:T(8,128)(2,1)} %param.23) | copy-start | bytes 460804
  10.6 297.4 %reduce-scatter.3.cloned.1.call-start = ((), (), s32[]{:S(2)}) async-start(), calls=%async_computation.7 | async-start | bytes 819200 | tf_op jit(solution)/shard_map/reduce_scatter | solution.py:257
  21.4 10.3 copy-start.14
  30.5 33.0 %copy-start.36 = (f32[960]{0:T(1024)}, f32[960]{0:T(1024)S(1)}, u32[]{:S(2)}) copy-start(f32[960]{0:T(1024)S(1)} %convert_element_type.108) | copy-start | bytes 11524
  31.2 32.2 %copy-start.38 = (f32[256]{0:T(256)}, f32[256]{0:T(256)S(1)}, u32[]{:S(2)}) copy-start(f32[256]{0:T(256)S(1)} %get-tuple-element.568) | copy-start | bytes 3076
  54.1 12.2 copy-start.29
  188.8 6.7 copy-start.26
  188.8 6.7 copy-start.28
  205.4 5.6 copy-start.2
  205.4 5.7 copy-start.21
  219.8 5.6 copy-start.2
  219.8 5.7 copy-start.21
  231.5 81.7 %reduce-scatter.5.cloned.1.call-start = ((), (), s32[]{:S(2)}) async-start(), calls=%async_computation.8 | async-start | bytes 819200 | tf_op jit(solution)/shard_map/reduce_scatter | solution.py:260
  233.3 5.9 copy-start.27
  246.5 607.1 %all-reduce.8.cloned.1.call-start = ((), (), s32[]{:S(2)}) async-start(), calls=%async_computation.10 | async-start | bytes 39329792
  246.6 10.4 copy-start.6
  304.8 8.4 copy-start.15
  313.2 6.0 copy-start.34
  323.5 27.1 %copy-start.17 = (bf16[4,76800]{1,0:T(4,128)(2,1)S(1)}, bf16[4,76800]{1,0:T(4,128)(2,1)}, u32[]{:S(2)}) copy-start(bf16[4,76800]{1,0:T(4,128)(2,1)} %reshape.463) | copy-start | bytes 1843204
  518.0 986.1 %all-gather.20.cloned.1.call-start = ((), (), s32[]{:S(2)}) async-start(), calls=%async_computation.9 | async-start | bytes 11063808 | tf_op jit(solution)/shard_map/all_gather | solution.py:306
  974.2 389.5 %copy-start.9 = (f32[256,960]{0,1:T(8,128)S(1)}, f32[256,960]{0,1:T(8,128)}, u32[]{:S(2)}) copy-start(f32[256,960]{0,1:T(8,128)} %copy-done.7) | copy-start | bytes 2949124
  1363.7 5.2 copy-start.4
  (31 other events, 91.7 us)
Sparse Core Ops, SparseCore 0:
  9.6 24.6 all-gather.9
  35.9 24.2 all-gather.11
  61.7 39.2 all-gather.13
  102.4 38.5 all-gather.15
  142.4 38.5 all-gather.17
  231.6 22.4 reduce-scatter.2
  256.6 22.4 reduce-scatter.4
  518.1 335.4 all-reduce.7
  1363.8 140.2 all-gather.19
where the time goes:
time: 1670 us; the launch traced here: 1650 us
  waiting for transfers between devices  539 us (32%)
  blocking collectives  428 us (26%)
  local copies, waits for them, and re-layouts  336 us (20%)
  other arithmetic  217 us (13%)
  matrix products  111 us (7%)
    unnamed x2, blocking collectives  391 us
    unnamed x10, waiting for transfers between devices  338 us
    unnamed x111, local copies, waits for them, and re-layouts  186 us
    all_gather x1, waiting for transfers between devices, body(): lax.all_gather(piece.astype(jnp.bfloat16), 'rep', axis=0, tiled=True)  134 us
    reshape x1, other arithmetic, body(): jnp.pad(shard_sum.reshape(-1), (0, padding)).reshape(replicas, piece_len)  108 us
    reshape x1, other arithmetic, body(): summed = whole.reshape(-1)[:width]  89.5 us
    concatenate x1, local copies, waits for them, and re-layouts, body(): packed = jnp.concatenate([grad.reshape(ways, -1) for grad in grads], axis=1)  47 us
    all_gather x1, waiting for transfers between devices, body(): lax.all_gather(w_down, 'fsdp', axis=0, tiled=True)  34.5 us
  transfers between devices with their start and end apart: 9, of which 4 were waited for; matrix products, arithmetic and copies ran while one was open for 9% of the time, Pallas kernels for 0%

commit v1 on v0

--- a/solution.py
+++ b/solution.py
@@ -1,6 +1,10 @@
+import functools
+
 import jax
 import jax.numpy as jnp
 from jax import lax
+from jax.experimental import pallas as pl
+from jax.experimental.pallas import tpu as pltpu
 from jax.sharding import PartitionSpec as P
 
 HEAD_DIM = 64
@@ -56,6 +60,260 @@
         scaled * values, axis=-1, keepdims=True
     )
     return (gain_part, input_part)
+
+
+MESH = pl.DeviceIdType.MESH
+
+
+def cut(extent, unit, most):
+    pieces = []
+    start = 0
+    while start < extent:
+        size = unit
+        while size * 2 <= min(most, extent - start):
+            size *= 2
+        pieces.append((start, size))
+        start += size
+    return pieces
+
+
+def row_block(rows):
+    for block in (80, 64, 48, 32, 16):
+        if rows % block == 0:
+            return block
+    return rows
+
+
+class Chunk:
+    def __init__(self, source, dim, rows, columns, owner_rows, bits):
+        self.source = source
+        self.dim = dim
+        self.rows = rows
+        self.columns = columns
+        self.owner_rows = owner_rows
+        unit = 128 if dim == 1 else 16
+        size = (rows[1], columns[1])[dim]
+        self.sizes = [size]
+        self.halved = []
+        for _ in range(bits):
+            half = size % (2 * unit) == 0
+            self.halved.append(half)
+            size = size // 2 if half else size
+            self.sizes.append(size)
+
+    def shape(self, level):
+        full = [self.rows[1], self.columns[1]]
+        full[self.dim] = self.sizes[level]
+        return tuple(full)
+
+
+def span(ref, dim, start, size):
+    unit = 128 if dim == 1 else 16
+    part = pl.ds(pl.multiple_of(start, unit), size)
+    return ref.at[:, part] if dim == 1 else ref.at[part, :]
+
+
+def add_into(target, other):
+    rows = target.shape[0]
+    block = row_block(rows)
+
+    def step(i, carry):
+        part = pl.ds(pl.multiple_of(i * block, 16), block)
+        total = target[part, :].astype(jnp.float32) + other[part, :].astype(jnp.float32)
+        target[part, :] = total.astype(target.dtype)
+        return carry
+
+    lax.fori_loop(0, rows // block, step, 0)
+
+
+def reduce_kernel(chunks, bits, *refs):
+    sources, gains = refs[:3], refs[3]
+    outs, gain_out = refs[4:7], refs[7]
+    scratch = list(refs[8:])
+    buffers = []
+    for chunk in chunks:
+        count = 4 + bits
+        buffers.append(scratch[:count])
+        scratch = scratch[count:]
+    gain_sum, gain_got, send_sem, recv_sem, local_sem, gain_send, gain_recv, out_sem = scratch
+    rep, fsdp = lax.axis_index("rep"), lax.axis_index("fsdp")
+    core, far = lax.rem(fsdp, 2), lax.div(fsdp, 2)
+    digits = [lax.rem(lax.div(rep, 2**k), 2) for k in range(bits)]
+    sibling = (rep, far * 2 + 1 - core)
+    across = (rep, (1 - far) * 2 + core)
+    peers = [(rep + (1 - 2 * digits[k]) * 2**k, fsdp) for k in range(bits)]
+    stages = [sibling, across] + peers
+
+    barrier = pltpu.get_barrier_semaphore()
+    for peer in stages:
+        pl.semaphore_signal(barrier, inc=1, device_id=peer, device_id_type=MESH)
+    pl.semaphore_wait(barrier, len(stages))
+
+    waiting = []
+    per_chunk = 3 + 2 * bits
+
+    def send(c, slot, src, dst, peer):
+        place = c * per_chunk + slot
+        copy = pltpu.make_async_remote_copy(
+            src_ref=src,
+            dst_ref=dst,
+            send_sem=send_sem.at[place],
+            recv_sem=recv_sem.at[place],
+            device_id=peer,
+            device_id_type=MESH,
+        )
+        copy.start()
+        waiting.append(copy)
+        return copy
+
+    def run_chunk(c, chunk):
+        own, near = buffers[c][0], buffers[c][1]
+        levels = buffers[c][2 : 3 + bits]
+        result = buffers[c][3 + bits]
+        source = sources[chunk.source]
+        columns = pl.ds(*chunk.columns)
+
+        def block(owner):
+            start = pl.multiple_of(owner * chunk.owner_rows + chunk.rows[0], 16)
+            return source.at[pl.ds(start, chunk.rows[1]), columns]
+
+        copies = [send(c, i, block(2 * i + 1 - core), near.at[i], sibling) for i in range(2)]
+        locals_ = []
+        for i in range(2):
+            copy = pltpu.make_async_copy(
+                block(2 * i + core), own.at[i], local_sem.at[2 * c + i]
+            )
+            copy.start()
+            locals_.append(copy)
+        yield
+        for copy in copies:
+            copy.wait_recv()
+        for copy in locals_:
+            copy.wait()
+        for i in range(2):
+            add_into(near.at[i], own.at[i])
+        copy = send(c, 2, near.at[1 - far], levels[0], across)
+        yield
+        copy.wait_recv()
+        add_into(levels[0], near.at[far])
+        offset = 0
+        offsets = []
+        for k in range(bits):
+            size = chunk.sizes[k + 1]
+            if chunk.halved[k]:
+                src = span(levels[k], chunk.dim, (1 - digits[k]) * size, size)
+                keep = span(levels[k], chunk.dim, digits[k] * size, size)
+                offset = offset + digits[k] * size
+            else:
+                src = keep = levels[k]
+            offsets.append(offset)
+            copy = send(c, 3 + k, src, levels[k + 1], peers[k])
+            yield
+            copy.wait_recv()
+            add_into(levels[k + 1], keep)
+        mine = span(result, chunk.dim, offset, chunk.sizes[bits])
+        mine[...] = levels[bits][...]
+        for k in reversed(range(bits)):
+            if not chunk.halved[k]:
+                continue
+            part = span(result, chunk.dim, offsets[k], chunk.sizes[k + 1])
+            copy = send(c, 3 + bits + k, part, part, peers[k])
+            yield
+            copy.wait_recv()
+        rows = pl.ds(*chunk.rows)
+        copy = pltpu.make_async_copy(
+            result, outs[chunk.source].at[rows, columns], out_sem.at[c]
+        )
+        copy.start()
+        locals_.append(copy)
+        final.append(copy)
+
+    final = []
+
+    def run_gains():
+        gain_sum[0] = gains[...]
+        for s, peer in enumerate(stages):
+            copy = pltpu.make_async_remote_copy(
+                src_ref=gain_sum.at[s],
+                dst_ref=gain_got.at[s],
+                send_sem=gain_send.at[s],
+                recv_sem=gain_recv.at[s],
+                device_id=peer,
+                device_id_type=MESH,
+            )
+            copy.start()
+            waiting.append(copy)
+            yield
+            copy.wait_recv()
+            gain_sum[s + 1] = gain_sum[s] + gain_got[s]
+        gain_out[...] = gain_sum[len(stages)]
+
+    todo = [run_chunk(c, chunk) for c, chunk in enumerate(chunks)] + [run_gains()]
+    active = []
+    while todo or active:
+        if todo:
+            active.insert(0, todo.pop(0))
+        left = []
+        for task in active:
+            try:
+                next(task)
+                left.append(task)
+            except StopIteration:
+                pass
+        active = left
+    for copy in waiting:
+        copy.wait_send()
+    for copy in final:
+        copy.wait()
+
+
+def reduce_grads(attn, ffn, down, gains):
+    ways = lax.axis_size("fsdp")
+    bits = lax.axis_size("rep").bit_length() - 1
+    chunks = []
+    for source, array in ((1, ffn), (0, attn)):
+        rows = array.shape[0] // ways
+        for part in cut(array.shape[1], 512, 2048):
+            chunks.append(Chunk(source, 1, (0, rows), part, rows, bits))
+    rows = down.shape[0] // ways
+    first = (rows * 3 // 5) // 16 * 16
+    for part in ((0, first), (first, rows - first)):
+        chunks.append(Chunk(2, 0, part, (0, down.shape[1]), rows, bits))
+    low = jnp.bfloat16
+    scratch = []
+    for chunk in chunks:
+        full = chunk.shape(0)
+        scratch += [pltpu.VMEM((2,) + full, low)] * 2
+        scratch += [pltpu.VMEM(chunk.shape(k), low) for k in range(bits + 1)]
+        scratch.append(pltpu.VMEM(full, low))
+    stages = bits + 2
+    per_chunk = 3 + 2 * bits
+    scratch += [
+        pltpu.VMEM((stages + 1,) + gains.shape, jnp.float32),
+        pltpu.VMEM((stages,) + gains.shape, jnp.float32),
+        pltpu.SemaphoreType.DMA((len(chunks) * per_chunk,)),
+        pltpu.SemaphoreType.DMA((len(chunks) * per_chunk,)),
+        pltpu.SemaphoreType.DMA((len(chunks) * 2,)),
+        pltpu.SemaphoreType.DMA((stages,)),
+        pltpu.SemaphoreType.DMA((stages,)),
+        pltpu.SemaphoreType.DMA((len(chunks),)),
+    ]
+    anywhere = pl.BlockSpec(memory_space=pl.ANY)
+    in_vmem = pl.BlockSpec(memory_space=pltpu.VMEM)
+    return pl.pallas_call(
+        functools.partial(reduce_kernel, chunks, bits),
+        out_shape=tuple(
+            jax.ShapeDtypeStruct((a.shape[0] // ways, a.shape[1]), low) for a in (attn, ffn, down)
+        )
+        + (jax.ShapeDtypeStruct(gains.shape, jnp.float32),),
+        in_specs=[anywhere] * 3 + [in_vmem],
+        out_specs=(anywhere,) * 3 + (in_vmem,),
+        scratch_shapes=scratch,
+        compiler_params=pltpu.CompilerParams(
+            collective_id=0, has_side_effects=True, vmem_limit_bytes=56 * 2**20
+        ),
+        name="reduce_grads",
+    )(attn, ffn, down, gains)
 
 
 def body(
@@ -72,7 +330,6 @@
     w_up,
     w_down,
 ):
-    shards = (norm1_gain, w_query, w_key, w_value, w_out, norm2_gain, w_gate, w_up, w_down)
     gathered = (
         lax.all_gather(norm1_gain, "fsdp", axis=0, tiled=True),
         lax.all_gather(w_query, "fsdp", axis=0, tiled=True),
@@ -183,37 +440,12 @@
     activated = gate * sigma
     hidden = (activated * up_proj).astype(jnp.bfloat16)
     mixed = (resid + matmul(hidden, down_weight)).astype(jnp.bfloat16)
-    again = (
-        lax.all_gather(norm1_gain, "fsdp", axis=0, tiled=True),
-        lax.all_gather(w_query, "fsdp", axis=0, tiled=True),
-        lax.all_gather(w_key, "fsdp", axis=0, tiled=True),
-        lax.all_gather(w_value, "fsdp", axis=0, tiled=True),
-        lax.all_gather(w_out, "fsdp", axis=0, tiled=True),
-        lax.all_gather(norm2_gain, "fsdp", axis=0, tiled=True),
-        lax.all_gather(w_gate, "fsdp", axis=0, tiled=True),
-        lax.all_gather(w_up, "fsdp", axis=0, tiled=True),
-        lax.all_gather(w_down, "fsdp", axis=0, tiled=True),
-    )
-    (
-        gain_one,
-        query_weight,
-        key_weight,
-        value_weight,
-        out_weight,
-        gain_two,
-        gate_weight,
-        up_weight,
-        down_weight,
-    ) = again
-    gain_one_f = gain_one.astype(jnp.float32)
-    gain_two_f = gain_two.astype(jnp.float32)
     upstream = cotangent.astype(jnp.float32)
     down_grad = left_inner(hidden, cotangent)
     hidden_back = right_inner(cotangent, down_weight)
     gate_back = (hidden_back * up_proj * sigma * (1.0 + gate * (1.0 - sigma))).astype(jnp.bfloat16)
     up_back = (hidden_back * activated).astype(jnp.bfloat16)
-    gate_grad = left_inner(normed_two, gate_back)
-    up_grad = left_inner(normed_two, up_back)
+    ffn_grad = left_inner(normed_two, jnp.concatenate([gate_back, up_back], axis=1))
     normed_two_back = right_inner(gate_back, gate_weight) + right_inner(up_back, up_weight)
     norm2_grad, resid_part = norm_back(resid, inverse_two, gain_two_f, normed_two_back)
     resid_back = upstream + resid_part
@@ -272,9 +504,7 @@
         .reshape(count, -1)
         .astype(jnp.bfloat16)
     )
-    query_grad = left_inner(normed_one, query_pre)
-    key_grad = left_inner(normed_one, key_pre)
-    value_grad = left_inner(normed_one, value_pre)
+    qkv_grad = left_inner(normed_one, jnp.concatenate([query_pre, key_pre, value_pre], axis=1))
     normed_one_back = (
         right_inner(query_pre, query_weight)
         + right_inner(key_pre, key_weight)
@@ -282,49 +512,33 @@
     )
     norm1_grad, input_part = norm_back(inputs, inverse_one, gain_one_f, normed_one_back)
     tokens_grad = (resid_back + input_part).astype(jnp.bfloat16)
-    grads = (
-        norm1_grad,
-        query_grad,
-        key_grad,
-        value_grad,
-        out_grad,
-        norm2_grad,
-        gate_grad,
-        up_grad,
-        down_grad,
-    )
-    packed = jnp.concatenate([grad.reshape(ways, -1) for grad in grads], axis=1)
-    width = packed.shape[1]
-    replicas = lax.axis_size("rep")
-    padding = -width % replicas
-    piece_len = (width + padding) // replicas
-    shard_sum = lax.psum_scatter(
-        packed.astype(jnp.bfloat16), "fsdp", scatter_dimension=0, tiled=True
-    ).astype(jnp.float32)
-    spread = jnp.pad(shard_sum.reshape(-1), (0, padding)).reshape(replicas, piece_len)
-    piece = lax.psum_scatter(spread, "rep", scatter_dimension=0, tiled=True)
-    whole = lax.all_gather(piece.astype(jnp.bfloat16), "rep", axis=0, tiled=True).astype(
-        piece.dtype
-    )
-    summed = whole.reshape(-1)[:width]
+    low = jnp.bfloat16
+    attn_grad = jnp.concatenate([qkv_grad.astype(low), out_grad.astype(low)], axis=1)
+    gains = jnp.stack([norm1_grad, norm2_grad])
+    gains = jnp.pad(gains, ((0, 6), (0, -gains.shape[1] % 128)))
+    attn_sum, ffn_sum, down_sum, gain_sum = reduce_grads(
+        attn_grad, ffn_grad.astype(low), down_grad.astype(low), gains
+    )
+    mine = lax.axis_index("fsdp") * norm1_gain.shape[0]
+    gain_rows = lax.dynamic_slice_in_dim(gain_sum, mine, norm1_gain.shape[0], axis=1)
     results = []
     offset = 0
-    for shard in shards:
-        size_here = shard.size
-        results.append(summed[offset : offset + size_here].reshape(shard.shape))
-        offset = offset + size_here
+    for shard in (w_query, w_key, w_value, w_out):
+        results.append(attn_sum[:, offset : offset + shard.shape[1]].astype(jnp.float32))
+        offset += shard.shape[1]
+    hidden_size = w_gate.shape[1]
     return (
         mixed,
         tokens_grad,
+        gain_rows[0],
         results[0],
         results[1],
         results[2],
         results[3],
-        results[4],
-        results[5],
-        results[6],
-        results[7],
-        results[8],
+        gain_rows[1],
+        ffn_sum[:, :hidden_size].astype(jnp.float32),
+        ffn_sum[:, hidden_size:].astype(jnp.float32),
+        down_sum.astype(jnp.float32),
     )
 
 

time: 1670 us -> 497 us (0.30); the launches traced: 1650 us -> 492 us
  waiting for transfers between devices: 539 us -> 85.2 us
  blocking collectives: 428 us -> 43.3 us
  local copies, waits for them, and re-layouts: 336 us -> 28.3 us
  other arithmetic: 217 us -> 32 us
  Pallas kernels: 0 us -> 183 us
    unnamed x2 -> x1, blocking collectives: 391 us -> 7.19 us
    unnamed x10 -> x7, waiting for transfers between devices: 338 us -> 3.15 us
    reshape x2 -> x0, other arithmetic: 197 us -> none  [the longest x1 108 us: body(): jnp.pad(shard_sum.reshape(-1), (0, padding)).reshape(replicas, piece_len)]
    pallas_call x0 -> x1, Pallas kernels: none -> 183 us  [reduce_grads(): pl.pallas_call(functools.partial(reduce_kernel, chunks, bits), out_shape=...]
    unnamed x111 -> x102, local copies, waits for them, and re-layouts: 186 us -> 11.5 us
    all_gather x1 -> x0, waiting for transfers between devices: 134 us -> none  [body(): lax.all_gather(piece.astype(jnp.bfloat16), 'rep', axis=0, tiled=True)]
    reshape x18 -> x0, local copies, waits for them, and re-layouts: 72.9 us -> none  [the longest x9 32.4 us: body(): packed = jnp.concatenate([grad.reshape(ways, -1) for grad in grads], axis=1)]
    concatenate x1 -> x0, local copies, waits for them, and re-layouts: 47 us -> none  [body(): packed = jnp.concatenate([grad.reshape(ways, -1) for grad in grads], axis=1)]
  transfers between devices with their start and end apart: 9 -> 7, of which waited for: 4 -> 3; matrix products, arithmetic and copies ran while one was open for 9% -> 18% of each run, Pallas kernels for 0% -> 0%
where the time goes in v1:
time: 497 us; the launch traced here: 492 us
  Pallas kernels  183 us (37%)
  matrix products  103 us (21%)
  waiting for transfers between devices  85.2 us (17%)
  blocking collectives  43.3 us (9%)
  other arithmetic  32 us (6%)
  local copies, waits for them, and re-layouts  28.3 us (6%)
  between operations  15.8 us (3%)
    pallas_call x1, Pallas kernels, reduce_grads(): pl.pallas_call(functools.partial(reduce_kernel, chunks, bits), out_shape=...  183 us
    all_gather x1, waiting for transfers between devices, body(): lax.all_gather(w_down, 'fsdp', axis=0, tiled=True)  34.6 us
    all_gather x1, waiting for transfers between devices, body(): lax.all_gather(w_up, 'fsdp', axis=0, tiled=True)  32.9 us
    dot_general x7, matrix products, matmul(): return jnp.dot(left, right, preferred_element_type=jnp.float32)  22.3 us
    dot_general x7, matrix products, right_inner(): lax.dot_general(left, right, (((1,), (1,)), ((), ())), preferred_element_...  21.3 us
    reduce_scatter x1, waiting for transfers between devices, body(): lax.psum_scatter(values_back_all.astype(jnp.bfloat16), 'fsdp', scatter_di...  14.5 us
    dot_general x4, matrix products, left_inner(): lax.dot_general(left, right, (((0,), (0,)), ((), ())), preferred_element_...  13.7 us
    dot_general x4, matrix products, scores_for(): jnp.einsum('bgrd,kgd->grbk', grouped, keys_here, preferred_element_type=j...  11.9 us
  transfers between devices with their start and end apart: 7, of which 3 were waited for; matrix products, arithmetic and copies ran while one was open for 18% of the time, Pallas kernels for 0%

profile of v1, /device:TPU:0, one launch (start us, length us, event | category | flops | bytes accessed | tf_op | source)
XLA Modules:
  0.0 491.5 jit_solution(2305172143843711774)
XLA Ops:
  10.8 9.3 %all-gather = bf16[4,240,320]{1,2,0:T(8,128)(2,1)S(1)} all-gather(bf16[1,240,320]{1,2,0:T(8,128)(2,1)S(1)} %bitcast.308), channel_id=1, replica_groups=mesh['rep'=8,'fsdp'=4] {'fsdp'}, dimensions={0}, use_global_device_ids=true | all-gather | bytes 768000 | tf_op jit(solution)/shard_map/all_gather | solution.py:337
  23.0 7.2 %all-reduce.3 = (bf16[960]{0:T(1024)(128)(2,1)S(1)}, bf16[960]{0:T(1024)(128)(2,1)S(1)}) all-reduce(bf16[960]{0:T(1024)(128)(2,1)S(1)} %dynamic-update-slice, bf16[960]{0:T(1024)(128)(2,1)S(1)} %dynamic-update-slice.1), channel_id=1, replica_groups=mesh['rep'=8,'fsdp'=4] {'fsdp'}, use_global_device_ids=true, to_apply=%add.1 | all-reduce | flops 1920 | bytes 7680
  31.4 7.3 %all_gather.35 = bf16[1024,320]{0,1:T(8,128)(2,1)S(1)} all-gather(bf16[256,320]{0,1:T(8,128)(2,1)S(1)} %convolution_convert_fusion.5), channel_id=1, replica_groups=mesh['rep'=8,'fsdp'=4] {'fsdp'}, dimensions={0}, use_global_device_ids=true | all-gather | bytes 819200 | tf_op jit(solution)/shard_map/all_gather | solution.py:378
  40.5 10.5 %all-gather.1 = bf16[4,240,320]{1,2,0:T(8,128)(2,1)S(1)} all-gather(bf16[1,240,320]{1,2,0:T(8,128)(2,1)S(1)} %bitcast.309), channel_id=1, replica_groups=mesh['rep'=8,'fsdp'=4] {'fsdp'}, dimensions={0}, use_global_device_ids=true | all-gather | bytes 768000 | tf_op jit(solution)/shard_map/all_gather | solution.py:336
  53.6 8.9 %all_gather.37 = bf16[1024,320]{0,1:T(8,128)(2,1)S(1)} all-gather(bf16[256,320]{0,1:T(8,128)(2,1)S(1)} %bitcast.296), channel_id=1, replica_groups=mesh['rep'=8,'fsdp'=4] {'fsdp'}, dimensions={0}, use_global_device_ids=true | all-gather | bytes 819200 | tf_op jit(solution)/shard_map/all_gather | solution.py:377
  66.0 20.8 %while.39 = (s32[]{:T(128)}, f32[5,3,256,1]{2,1,0,3:T(4,128)S(1)}, f32[5,3,256,1]{2,1,0,3:T(4,128)S(1)}, s32[2,512]{1,0:T(2,128)S(1)}, s32[2,512]{1,0:T(2,128)S(...) while((s32[]{:T(128)}, f32[5,3,256,1]{2,1,0,3:T(4,128)S(1)}, ...), condition=%wide.region_7.8_spmd.clone, body=%wide.region_4.7_spmd.clone.sunk | while | flops 267799552 | bytes 17156236 | solution.py:412
  66.3 5.0 %fusion.164 = (f32[5,3,256]{2,1,0:T(4,128)S(1)}, f32[5,512,256,3]{2,1,3,0:T(8,128)}) fusion(pred[256,512]{0,1:T(8,128)(4,1)S(1)} %compare_and_fusion.6, bf16[256,5,3,64]{0,3,2,1:T(8,128)(2,1)S(1)} %get-tuple-element.883, bf16[2,512,5,64]{1,3,2,0:T(8,128)(2,1)S(1)} %get-tuple-element.882, s32[]{:T(128)S(6)} %copy.122), kind=kOutput, calls=%fused_computation.5.clone.1 | convolution fusion | flops 257552640 | bytes 8829956 | tf_op jit(solution)/shard_map/while/body/eval_jaxpr/bgrd,kgd->grbk/dot_general | solution.py:395
  71.3 5.5 %select_reduce_fusion.3 = f32[5,3,256]{2,1,0:T(4,128)S(1)} fusion(f32[5,512,256,3]{2,1,3,0:T(8,128)} %get-tuple-element.825, f32[5,3,256]{2,1,0:T(4,128)S(1)} %bitcast.283, pred[256,512]{0,1:T(8,128)(4,1)S(1)} %compare_and_fusion.6), kind=kLoop, calls=%fused_computation.4.clone.1 | loop fusion | flops 9826560 | bytes 8026112 | tf_op jit(solution)/shard_map/while/body/eval_jaxpr/reduce_sum | solution.py:406
  77.1 4.5 fusion.164
  81.6 5.2 %select_reduce_fusion.3 = f32[5,3,256]{2,1,0:T(4,128)S(1)} fusion(f32[5,512,256,3]{2,1,3,0:T(8,128)} %get-tuple-element.825, f32[5,3,256]{2,1,0:T(4,128)S(1)} %bitcast.283, pred[256,512]{0,1:T(8,128)(4,1)S(1)} %compare_and_fusion.6), kind=kLoop, calls=%fused_computation.4.clone.1 | loop fusion | flops 9826560 | bytes 8026112 | tf_op jit(solution)/shard_map/while/body/eval_jaxpr/reduce_sum | solution.py:406
  86.8 10.2 %while.40 = (s32[]{:T(128)}, f32[256,5,3,64]{0,3,2,1:T(8,128)}, bf16[2,512,5,64]{1,3,2,0:T(8,128)(2,1)}, s32[2,512]{1,0:T(2,128)S(1)}, s32[2,512]{1,0:T(2,128)S(...) while((s32[]{:T(128)}, f32[256,5,3,64]{0,3,2,1:T(8,128)}, ...), condition=%wide.region_9.10_spmd.clone, body=%wide.region_8.9_spmd.clone.sunk | while | flops 514031872 | bytes 3412622 | solution.py:428
  87.1 4.6 fusion.169
  91.9 5.0 %fusion.169 = f32[256,5,3,64]{0,3,2,1:T(8,128)} fusion(f32[5,3,256]{2,1,0:T(4,128)S(1)} %bitcast.311, pred[256,512]{0,1:T(8,128)(4,1)S(1)} %compare_and_fusion.7, bf16[256,5,3,64]{0,3,2,1:T(8,128)(2,1)S(1)} %get-tuple-element.918, f32[256,5,3,64]{0,3,2,1:T(8,128)} %get-tuple-element.900, pred[]{:T(512)S(6)} %compare.21, ...), kind=kOutput, calls=%fused_computation.26.clone.1 | convolution fusion | flops 513638400 | bytes 3266048 | tf_op jit(solution)/shard_map/while/body/eval_jaxpr/grbk,kgd->bgrd/dot_general | solution.py:424
  102.2 5.6 %fusion.101 = f32[256,2560]{1,0:T(8,128)} fusion(bf16[256,960]{0,1:T(8,128)(2,1)S(1)} %multiply_convert_fusion.3, bf16[960,2560]{1,0:T(8,128)(2,1)} %all-gather.12.cloned.1.call-done), kind=kOutput, calls=%fused_computation.171 | convolution fusion | flops 1258291200 | bytes 8028160 | tf_op jit(solution)/shard_map/dot_general | solution.py:41
  107.8 32.9 %all-gather.14.cloned.1.call-done = bf16[960,2560]{1,0:T(8,128)(2,1)} async-done(((bf16[240,2560]{1,0:T(8,128)(2,1)}), bf16[960,2560]{1,0:T(8,128)(2,1)}) %all-gather.14.cloned.1.call-update) | async-done | bytes 4915216 | tf_op jit(solution)/shard_map/all_gather | solution.py:341
  140.7 5.4 %fusion.102 = f32[256,2560]{1,0:T(8,128)} fusion(bf16[256,960]{0,1:T(8,128)(2,1)S(1)} %multiply_convert_fusion.3, bf16[960,2560]{1,0:T(8,128)(2,1)} %all-gather.14.cloned.1.call-done), kind=kOutput, calls=%fused_computation.172 | convolution fusion | flops 1258291200 | bytes 8028160 | tf_op jit(solution)/shard_map/dot_general | solution.py:41
  146.2 34.6 %all-gather.16.cloned.1.call-done = bf16[2560,960]{0,1:T(8,128)(2,1)} async-done(((bf16[640,960]{0,1:T(8,128)(2,1)}), bf16[2560,960]{0,1:T(8,128)(2,1)}) %all-gather.16.cloned.1.call-update) | async-done | bytes 4915216 | tf_op jit(solution)/shard_map/all_gather | solution.py:342
  180.7 7.6 %multiply_convert_fusion = (bf16[256,2560]{1,0:T(8,128)(2,1)S(1)}, bf16[256,2560]{1,0:T(8,128)(2,1)S(1)}, bf16[256,2560]{1,0:T(8,128)(2,1)}) fusion(f32[256,2560]{1,0:T(8,128)} %fusion.101, f32[256,2560]{1,0:T(8,128)} %fusion.102, bf16[256,960]{0,1:T(8,128)(2,1)S(1)} %copy-done.15, bf16[2560,960]{0,1:T(8,128)(2,1)} %all-gather.16.cloned.1.call-done), kind=kOutput, calls=%fused_computation.81 | convolution fusion | flops 1268121600 | bytes 14581760 | tf_op jit(solution)/shard_map/dot_general | solution.py:51
  188.3 4.8 fusion.103
  198.8 29.4 %while.41 = (s32[]{:T(128)}, f32[256,5,3,64]{0,3,2,1:T(8,128)S(1)}, bf16[2,512,5,64]{1,3,2,0:T(8,128)(2,1)}, bf16[2,512,5,64]{1,3,2,0:T(8,128)(2,1)}, bf16[2,512...) while((s32[]{:T(128)}, f32[256,5,3,64]{0,3,2,1:T(8,128)S(1)}, ...), condition=%wide.region_14.15_spmd.clone, body=%wide.region_13.14_spmd.clone.sunk | while | flops 1282932992 | bytes 127277416 | solution.py:483
  200.5 4.1 fusion.181
  204.7 3.1 fusion.182
  215.2 4.1 fusion.181
  234.9 3.8 convolution_convert_fusion.1
  238.7 5.6 %convolution_convert_fusion.refs_1_ = bf16[960,5120]{1,0:T(8,128)(2,1)} fusion(bf16[256,960]{0,1:T(8,128)(2,1)S(1)} %copy-done.4, bf16[256,2560]{1,0:T(8,128)(2,1)S(1)} %copy-done.29, bf16[256,2560]{1,0:T(8,128)(2,1)S(1)} %copy-done.31), kind=kOutput, calls=%fused_computation.74 | convolution fusion | flops 2526740480 | bytes 12943360 | tf_op jit(solution)/shard_map/dot_general | solution.py:45
  244.3 3.2 fusion.104
  247.5 8.0 %copy.98.refs_2_ = bf16[2560,960]{1,0:T(8,128)(2,1)} copy(bf16[2560,960]{0,1:T(8,128)(2,1)} %convolution_convert_fusion.1) | data formatting | bytes 9830400 | tf_op jit(solution)/shard_map/convert_element_type | solution.py:520
  255.4 5.1 %fusion.73 = bf16[256,960]{0,1:T(8,128)(2,1)} fusion(f32[256,960]{0,1:T(8,128)S(1)} %copy-done.12, bf16[256,2560]{1,0:T(8,128)(2,1)} %get-tuple-element.609, bf16[2560,960]{0,1:T(8,128)(2,1)} %all-gather.16.cloned.1.call-done), kind=kOutput, calls=%fused_computation.98 | convolution fusion | flops 1258782720 | bytes 7700480 | tf_op jit(solution)/shard_map/dot_general | solution.py:41
  264.2 14.5 %reduce-scatter.5.cloned.1.call-done = bf16[256,320]{0,1:T(8,128)(2,1)} async-done(((bf16[1024,320]{0,1:T(8,128)(2,1)}), bf16[256,320]{0,1:T(8,128)(2,1)}) %reduce-scatter.5.cloned.1.call-update) | async-done | bytes 163856 | tf_op jit(solution)/shard_map/reduce_scatter | solution.py:492
  281.2 3.6 pad_maximum_fusion.refs_0_
  286.1 182.8 %reduce_grads.1 = (bf16[240,2560]{1,0:T(8,128)(2,1)}, bf16[240,5120]{1,0:T(8,128)(2,1)}, bf16[640,960]{1,0:T(8,128)(2,1)}, f32[8,1024]{1,0:T(8,128)}) custom-call(bf16[960,2560]{1,0:T(8,128)(2,1)} %pad_maximum_fusion.refs_0_, bf16[960,5120]{1,0:T(8,128)(2,1)} %convolution_convert_fusion.refs_1_, bf16[2560,960]{1,0:T(8,128)(2,1)} %copy.98.refs_2_, ...), custom_call_target="tpu_custom_call" | custom-call | tf_op jit(solution)/shard_map/reduce_grads/pallas_call | solution.py:303
  474.6 4.6 slice_convert_fusion
  (235 shorter events, 68.7 us)
Async XLA Ops:
  7.2 56.0 %all-gather.8.cloned.1.call-start = ((), (), s32[]{:S(2)}) async-start(), calls=%async_computation.2 | async-start | bytes 2457600 | tf_op jit(solution)/shard_map/all_gather | solution.py:335
  7.9 13.3 %copy-start.49 = (u32[32]{0:T(128)S(1)}, u32[32]{0:T(128)}, u32[]{:S(2)}) copy-start(u32[32]{0:T(128)} %constant.103) | copy-start | bytes 388
  7.9 14.6 %copy-start.46 = (bf16[240]{0:T(256)(128)(2,1)S(1)}, bf16[240]{0:T(256)(128)(2,1)}, u32[]{:S(2)}) copy-start(bf16[240]{0:T(256)(128)(2,1)} %param.21) | copy-start | bytes 1444
  7.9 14.8 %copy-start.47 = (bf16[240]{0:T(256)(128)(2,1)S(1)}, bf16[240]{0:T(256)(128)(2,1)}, u32[]{:S(2)}) copy-start(bf16[240]{0:T(256)(128)(2,1)} %param.26) | copy-start | bytes 1444
  8.0 22.3 %copy-start.7 = (bf16[256,960]{0,1:T(8,128)(2,1)S(1)}, bf16[256,960]{0,1:T(8,128)(2,1)}, u32[]{:S(2)}) copy-start(bf16[256,960]{0,1:T(8,128)(2,1)} %param.18) | copy-start | bytes 1474564
  8.0 90.4 %all-gather.10.cloned.1.call-start = ((), (), s32[]{:S(2)}) async-start(), calls=%async_computation.3 | async-start | bytes 2457600 | tf_op jit(solution)/shard_map/all_gather | solution.py:338
  8.7 93.4 %all-gather.12.cloned.1.call-start = ((), (), s32[]{:S(2)}) async-start(), calls=%async_computation.4 | async-start | bytes 6144000 | tf_op jit(solution)/shard_map/all_gather | solution.py:340
  9.5 131.3 %all-gather.14.cloned.1.call-start = ((), (), s32[]{:S(2)}) async-start(), calls=%async_computation.5 | async-start | bytes 6144000 | tf_op jit(solution)/shard_map/all_gather | solution.py:341
  10.0 170.7 %all-gather.16.cloned.1.call-start = ((), (), s32[]{:S(2)}) async-start(), calls=%async_computation.6 | async-start | bytes 6144000 | tf_op jit(solution)/shard_map/all_gather | solution.py:342
  10.6 249.9 %reduce-scatter.3.cloned.1.call-start = ((), (), s32[]{:S(2)}) async-start(), calls=%async_computation.7 | async-start | bytes 819200 | tf_op jit(solution)/shard_map/reduce_scatter | solution.py:489
  20.1 20.0 %copy-start.48 = (s32[1,8]{1,0:T(1,128)S(1)}, s32[1,8]{1,0:T(1,128)}, u32[]{:S(2)}) copy-start(s32[1,8]{1,0:T(1,128)} %param.20) | copy-start | bytes 100
  20.1 20.4 %copy-start.40 = (bf16[240,320]{0,1:T(8,128)(2,1)S(1)}, bf16[240,320]{0,1:T(8,128)(2,1)}, u32[]{:S(2)}) copy-start(bf16[240,320]{0,1:T(8,128)(2,1)} %param.23) | copy-start | bytes 460804
  21.2 10.3 %copy-start.18 = (bf16[960,320]{0,1:T(8,128)(2,1)}, bf16[960,320]{0,1:T(8,128)(2,1)S(1)}, u32[]{:S(2)}) copy-start(bf16[960,320]{0,1:T(8,128)(2,1)S(1)} %reshape.398) | copy-start | bytes 1843204
  30.2 32.9 %copy-start.41 = (f32[960]{0:T(1024)}, f32[960]{0:T(1024)S(1)}, u32[]{:S(2)}) copy-start(f32[960]{0:T(1024)S(1)} %convert_element_type.135) | copy-start | bytes 11524
  31.0 32.2 %copy-start.43 = (f32[256]{0:T(256)}, f32[256]{0:T(256)S(1)}, u32[]{:S(2)}) copy-start(f32[256]{0:T(256)S(1)} %get-tuple-element.630) | copy-start | bytes 3076
  53.5 12.4 %copy-start.33 = (f32[256,32]{0,1:T(8,128)}, f32[256,32]{0,1:T(8,128)S(1)}, u32[]{:S(2)}) copy-start(f32[256,32]{0,1:T(8,128)S(1)} %get-tuple-element.628) | copy-start | bytes 98308
  102.1 38.6 %copy-start.3 = (bf16[256,960]{0,1:T(8,128)(2,1)}, bf16[256,960]{0,1:T(8,128)(2,1)S(1)}, u32[]{:S(2)}) copy-start(bf16[256,960]{0,1:T(8,128)(2,1)S(1)} %multiply_convert_fusion.3) | copy-start | bytes 1474564
  107.8 72.9 %copy-start.15 = (bf16[256,960]{0,1:T(8,128)(2,1)S(1)}, bf16[256,960]{0,1:T(8,128)(2,1)}, u32[]{:S(2)}) copy-start(bf16[256,960]{0,1:T(8,128)(2,1)} %param.19) | copy-start | bytes 1474564
  188.3 4.9 copy-start.5
  188.3 5.1 %copy-start.11 = (f32[256,960]{0,1:T(8,128)S(1)}, f32[256,960]{0,1:T(8,128)}, u32[]{:S(2)}) copy-start(f32[256,960]{0,1:T(8,128)} %copy-done.10) | copy-start | bytes 2949124
  204.7 5.6 %copy-start.2 = (f32[5,512,256,3]{2,1,3,0:T(8,128)S(1)}, f32[5,512,256,3]{2,1,3,0:T(8,128)}, u32[]{:S(2)}) copy-start(f32[5,512,256,3]{2,1,3,0:T(8,128)} %copy-done.1) | copy-start | bytes 23592964 | tf_op jit(solution)/shard_map/while
  219.3 5.6 %copy-start.2 = (f32[5,512,256,3]{2,1,3,0:T(8,128)S(1)}, f32[5,512,256,3]{2,1,3,0:T(8,128)}, u32[]{:S(2)}) copy-start(f32[5,512,256,3]{2,1,3,0:T(8,128)} %copy-done.1) | copy-start | bytes 23592964 | tf_op jit(solution)/shard_map/while
  228.3 6.6 %copy-start.17 = (bf16[256,960]{0,1:T(8,128)(2,1)S(1)}, bf16[256,960]{0,1:T(8,128)(2,1)}, u32[]{:S(2)}) copy-start(bf16[256,960]{0,1:T(8,128)(2,1)} %param.19) | copy-start | bytes 1474564
  231.1 47.6 %reduce-scatter.5.cloned.1.call-start = ((), (), s32[]{:S(2)}) async-start(), calls=%async_computation.8 | async-start | bytes 819200 | tf_op jit(solution)/shard_map/reduce_scatter | solution.py:492
  238.7 5.6 %copy-start.36 = (bf16[256,15,64]{0,2,1:T(8,128)(2,1)S(1)}, bf16[256,15,64]{0,2,1:T(8,128)(2,1)}, u32[]{:S(2)}) copy-start(bf16[256,15,64]{0,2,1:T(8,128)(2,1)} %pad_maximum_fusion.2) | copy-start | bytes 1474564
  247.5 8.0 %copy-start.12 = (f32[256,960]{0,1:T(8,128)S(1)}, f32[256,960]{0,1:T(8,128)}, u32[]{:S(2)}) copy-start(f32[256,960]{0,1:T(8,128)} %copy-done.10) | copy-start | bytes 2949124
  255.4 6.1 %copy-start.21 = (bf16[960,320]{0,1:T(8,128)(2,1)S(1)}, bf16[960,320]{0,1:T(8,128)(2,1)}, u32[]{:S(2)}) copy-start(bf16[960,320]{0,1:T(8,128)(2,1)} %copy-done.20) | copy-start | bytes 1843204
  260.6 18.2 %copy-start.42 = (f32[960]{0:T(1024)S(1)}, f32[960]{0:T(1024)}, u32[]{:S(2)}) copy-start(f32[960]{0:T(1024)} %copy-done.41) | copy-start | bytes 11524
  260.6 18.2 %copy-start.44 = (f32[256]{0:T(256)S(1)}, f32[256]{0:T(256)}, u32[]{:S(2)}) copy-start(f32[256]{0:T(256)} %copy-done.43) | copy-start | bytes 3076
  264.2 16.9 %copy-start.6 = (bf16[960,960]{1,0:T(8,128)(2,1)S(1)}, bf16[960,960]{1,0:T(8,128)(2,1)}, u32[]{:S(2)}) copy-start(bf16[960,960]{1,0:T(8,128)(2,1)} %convolution_convert_fusion.3) | copy-start | bytes 5529604
  474.6 7.4 %copy-start.9 = (bf16[256,960]{0,1:T(8,128)(2,1)S(1)}, bf16[256,960]{0,1:T(8,128)(2,1)}, u32[]{:S(2)}) copy-start(bf16[256,960]{0,1:T(8,128)(2,1)} %param.18) | copy-start | bytes 1474564
  474.6 7.4 %copy-start.45 = (f32[256]{0:T(256)S(1)}, f32[256]{0:T(256)}, u32[]{:S(2)}) copy-start(f32[256]{0:T(256)} %get-tuple-element.629) | copy-start | bytes 3076
  (31 other events, 91.5 us)
Sparse Core Ops, SparseCore 0:
  9.6 24.7 all-gather.7
  35.9 23.7 all-gather.9
  61.3 39.3 all-gather.11
  102.1 38.5 all-gather.13
  142.2 38.5 all-gather.15
  231.2 22.4 reduce-scatter.2
  256.2 22.4 reduce-scatter.4

commit v2 on v1

--- a/solution.py
+++ b/solution.py
@@ -63,6 +63,34 @@
 
 
 MESH = pl.DeviceIdType.MESH
+
+
+MOST = 512
+GATHER_MOST = 1024
+REDUCE_AHEAD = 1
+GATHER_AHEAD = 1
+
+
+def run_staggered(todo, ahead):
+    active = []
+    early = []
+    while todo or early or active:
+        while todo and len(early) < ahead:
+            early.append(todo.pop(0))
+            next(early[-1])
+        if early:
+            active.insert(0, early.pop(0))
+        if todo:
+            early.append(todo.pop(0))
+            next(early[-1])
+        left = []
+        for task in active:
+            try:
+                next(task)
+                left.append(task)
+            except StopIteration:
+                pass
+        active = left
 
 
 def cut(extent, unit, most):
@@ -249,18 +277,7 @@
         gain_out[...] = gain_sum[len(stages)]
 
     todo = [run_chunk(c, chunk) for c, chunk in enumerate(chunks)] + [run_gains()]
-    active = []
-    while todo or active:
-        if todo:
-            active.insert(0, todo.pop(0))
-        left = []
-        for task in active:
-            try:
-                next(task)
-                left.append(task)
-            except StopIteration:
-                pass
-        active = left
+    run_staggered(todo, REDUCE_AHEAD)
     for copy in waiting:
         copy.wait_send()
     for copy in final:
@@ -273,11 +290,10 @@
     chunks = []
     for source, array in ((1, ffn), (0, attn)):
         rows = array.shape[0] // ways
-        for part in cut(array.shape[1], 512, 2048):
+        for part in cut(array.shape[1], 512, MOST):
             chunks.append(Chunk(source, 1, (0, rows), part, rows, bits))
     rows = down.shape[0] // ways
-    first = (rows * 3 // 5) // 16 * 16
-    for part in ((0, first), (first, rows - first)):
+    for part in cut(rows, 128, 256):
         chunks.append(Chunk(2, 0, part, (0, down.shape[1]), rows, bits))
     low = jnp.bfloat16
     scratch = []
@@ -316,6 +332,112 @@
     )(attn, ffn, down, gains)
 
 
+def gather_kernel(plan, *refs):
+    count = len({item[0] for item in plan})
+    shards, outs = refs[:count], refs[count : 2 * count]
+    send_sem, recv_sem, local_sem = refs[2 * count :]
+    rep, fsdp = lax.axis_index("rep"), lax.axis_index("fsdp")
+    core, far = lax.rem(fsdp, 2), lax.div(fsdp, 2)
+    half = lax.rem(rep, 2)
+    other = (1 - far) * 2 + core
+    sibling = (rep, far * 2 + 1 - core)
+    across = (rep, other)
+    twin = (rep + 1 - 2 * half, fsdp)
+
+    barrier = pltpu.get_barrier_semaphore()
+    for peer in (sibling, across, twin):
+        pl.semaphore_signal(barrier, inc=1, device_id=peer, device_id_type=MESH)
+    pl.semaphore_wait(barrier, 3)
+
+    waiting = []
+
+    def send(c, slot, src, dst, peer):
+        copy = pltpu.make_async_remote_copy(
+            src_ref=src,
+            dst_ref=dst,
+            send_sem=send_sem.at[c * 5 + slot],
+            recv_sem=recv_sem.at[c * 5 + slot],
+            device_id=peer,
+            device_id_type=MESH,
+        )
+        copy.start()
+        waiting.append(copy)
+        return copy
+
+    def run_chunk(c, item):
+        which, dim, start, size = item
+        shard, out = shards[which], outs[which]
+        height = shard.shape[0]
+
+        def view(ref, owner, part):
+            begin, extent = start, size
+            if part is not None:
+                extent = size // 2
+                begin = start + part * extent
+            if dim == 0:
+                first = begin if owner is None else owner * height + begin
+                return ref.at[pl.ds(pl.multiple_of(first, 16), extent), :]
+            first = 0 if owner is None else pl.multiple_of(owner * height, 16)
+            return ref.at[pl.ds(first, height), pl.ds(pl.multiple_of(begin, 128), extent)]
+
+        over = send(
+            c, 0, view(shard, None, half), view(out, fsdp, half), across
+        )
+        near = [send(c, 1, view(shard, None, None), view(out, fsdp, None), sibling)]
+        keep = pltpu.make_async_copy(
+            view(shard, None, None), view(out, fsdp, None), local_sem.at[c]
+        )
+        keep.start()
+        yield
+        over.wait_recv()
+        got = view(out, other, half)
+        swap = send(c, 2, got, got, twin)
+        near.append(send(c, 3, got, got, sibling))
+        yield
+        swap.wait_recv()
+        rest = view(out, other, 1 - half)
+        near.append(send(c, 4, rest, rest, sibling))
+        yield
+        for copy in near:
+            copy.wait_recv()
+        keep.wait()
+
+    todo = [run_chunk(c, item) for c, item in enumerate(plan)]
+    run_staggered(todo, GATHER_AHEAD)
+    for copy in waiting:
+        copy.wait_send()
+
+
+def gather_weights(arrays):
+    ways = lax.axis_size("fsdp")
+    plan = []
+    for i, array in enumerate(arrays):
+        if array.shape[1] % 256 == 0:
+            parts = [(i, 1, a, b) for a, b in cut(array.shape[1], 256, GATHER_MOST)]
+        else:
+            step = array.shape[0] // 2
+            parts = [(i, 0, 0, step), (i, 0, step, step)]
+        plan += parts
+    anywhere = pl.BlockSpec(memory_space=pl.ANY)
+    return pl.pallas_call(
+        functools.partial(gather_kernel, plan),
+        out_shape=tuple(
+            jax.ShapeDtypeStruct((a.shape[0] * ways, a.shape[1]), a.dtype) for a in arrays
+        ),
+        in_specs=[pl.BlockSpec(memory_space=pltpu.VMEM)] * len(arrays),
+        out_specs=(anywhere,) * len(arrays),
+        scratch_shapes=[
+            pltpu.SemaphoreType.DMA((len(plan) * 5,)),
+            pltpu.SemaphoreType.DMA((len(plan) * 5,)),
+            pltpu.SemaphoreType.DMA((len(plan),)),
+        ],
+        compiler_params=pltpu.CompilerParams(
+            collective_id=1, has_side_effects=True, vmem_limit_bytes=32 * 2**20
+        ),
+        name="gather_weights",
+    )(*arrays)
+
+
 def body(
     tokens,
     cotangent,
@@ -330,28 +452,19 @@
     w_up,
     w_down,
 ):
-    gathered = (
-        lax.all_gather(norm1_gain, "fsdp", axis=0, tiled=True),
-        lax.all_gather(w_query, "fsdp", axis=0, tiled=True),
-        lax.all_gather(w_key, "fsdp", axis=0, tiled=True),
-        lax.all_gather(w_value, "fsdp", axis=0, tiled=True),
-        lax.all_gather(w_out, "fsdp", axis=0, tiled=True),
-        lax.all_gather(norm2_gain, "fsdp", axis=0, tiled=True),
-        lax.all_gather(w_gate, "fsdp", axis=0, tiled=True),
-        lax.all_gather(w_up, "fsdp", axis=0, tiled=True),
-        lax.all_gather(w_down, "fsdp", axis=0, tiled=True),
-    )
-    (
-        gain_one,
-        query_weight,
-        key_weight,
-        value_weight,
-        out_weight,
-        gain_two,
-        gate_weight,
-        up_weight,
-        down_weight,
-    ) = gathered
+    gains = jnp.stack([norm1_gain, norm2_gain])
+    gains = jnp.pad(gains, ((0, 14), (0, -gains.shape[1] % 256)))
+    attn_shard = jnp.concatenate([w_query, w_key, w_value, w_out], axis=1)
+    attn_weight, gate_weight, up_weight, down_weight, all_gains = gather_weights(
+        [attn_shard, w_gate, w_up, w_down, gains]
+    )
+    width = w_query.shape[0]
+    all_gains = all_gains.reshape(-1, 16, all_gains.shape[1])[:, :2, :width]
+    gain_one, gain_two = all_gains[:, 0].reshape(-1), all_gains[:, 1].reshape(-1)
+    splits = [w_query.shape[1], w_key.shape[1], w_value.shape[1]]
+    key_at, value_at, out_at = splits[0], sum(splits[:2]), sum(splits)
+    qkv_weight = attn_weight[:, :out_at]
+    out_weight = attn_weight[:, out_at:]
     count = tokens.shape[0]
     ways = lax.axis_size("fsdp")
     total = count * ways
@@ -366,13 +479,14 @@
     inverse_one = lax.rsqrt(jnp.mean(inputs * inputs, axis=-1, keepdims=True) + EPS)
     gain_one_f = gain_one.astype(jnp.float32)
     normed_one = (inputs * inverse_one * gain_one_f).astype(jnp.bfloat16)
+    qkv = matmul(normed_one, qkv_weight)
     query = rotate(
-        matmul(normed_one, query_weight).reshape(count, -1, head_dim), position_mine, 1.0
+        qkv[:, :key_at].reshape(count, -1, head_dim), position_mine, 1.0
     ).astype(jnp.bfloat16)
     key_local = rotate(
-        matmul(normed_one, key_weight).reshape(count, -1, head_dim), position_mine, 1.0
+        qkv[:, key_at:value_at].reshape(count, -1, head_dim), position_mine, 1.0
     ).astype(jnp.bfloat16)
-    value_local = matmul(normed_one, value_weight).astype(jnp.bfloat16)
+    value_local = qkv[:, value_at:].astype(jnp.bfloat16)
     all_keys, all_values = (
         lax.all_gather(key_local.reshape(count, -1), "fsdp", axis=0, tiled=True),
         lax.all_gather(value_local, "fsdp", axis=0, tiled=True),
@@ -504,12 +618,9 @@
         .reshape(count, -1)
         .astype(jnp.bfloat16)
     )
-    qkv_grad = left_inner(normed_one, jnp.concatenate([query_pre, key_pre, value_pre], axis=1))
-    normed_one_back = (
-        right_inner(query_pre, query_weight)
-        + right_inner(key_pre, key_weight)
-        + right_inner(value_pre, value_weight)
-    )
+    qkv_pre = jnp.concatenate([query_pre, key_pre, value_pre], axis=1)
+    qkv_grad = left_inner(normed_one, qkv_pre)
+    normed_one_back = right_inner(qkv_pre, qkv_weight)
     norm1_grad, input_part = norm_back(inputs, inverse_one, gain_one_f, normed_one_back)
     tokens_grad = (resid_back + input_part).astype(jnp.bfloat16)
     low = jnp.bfloat16

time: 497 us -> 457 us (0.920)
  waiting for transfers between devices: 85.2 us -> 13.1 us
  Pallas kernels: 183 us -> 226 us
  blocking collectives: 43.3 us -> 16.3 us
  local copies, waits for them, and re-layouts: 28.3 us -> 47 us
  matrix products: 103 us -> 95.3 us
  other arithmetic: 32 us -> 37.1 us
    pallas_call x0 -> x1, Pallas kernels: none -> 70.6 us  [gather_weights(): pl.pallas_call(functools.partial(gather_kernel, plan), out_shape=tuple((j...]
    all_gather x5 -> x0, waiting for transfers between devices: 67.6 us -> none  [the longest x1 34.6 us: body(): lax.all_gather(w_down, 'fsdp', axis=0, tiled=True)]
    pallas_call x1, Pallas kernels: 183 us -> 156 us  [reduce_grads(): pl.pallas_call(functools.partial(reduce_kernel, chunks, bits), out_shape=...]
    all_gather x2 -> x0, blocking collectives: 19.8 us -> none  [the longest x1 10.5 us: body(): lax.all_gather(w_key, 'fsdp', axis=0, tiled=True)]
    unnamed x102 -> x94, local copies, waits for them, and re-layouts: 11.5 us -> 24 us
    dot_general x7 -> x5, matrix products: 21.3 us -> 13.8 us  [right_inner(): lax.dot_general(left, right, (((1,), (1,)), ((), ())), preferred_element_...]
    unnamed x1 -> x0, blocking collectives: 7.19 us -> none
    dot_general x7 -> x5, matrix products: 22.3 us -> 20.2 us  [matmul(): return jnp.dot(left, right, preferred_element_type=jnp.float32)]
  transfers between devices with their start and end apart: 7 -> 2, of which waited for: 3 -> 1; matrix products, arithmetic and copies ran while one was open for 18% -> 8% of each run, Pallas kernels for 0% -> 0%
where the time goes in v2:
time: 457 us; the launch traced here: 451 us
  Pallas kernels  226 us (49%)
  matrix products  95.3 us (21%)
  local copies, waits for them, and re-layouts  47 us (10%)
  other arithmetic  37.1 us (8%)
  blocking collectives  16.3 us (4%)
  between operations  14.9 us (3%)
  waiting for transfers between devices  13.1 us (3%)
    pallas_call x1, Pallas kernels, reduce_grads(): pl.pallas_call(functools.partial(reduce_kernel, chunks, bits), out_shape=...  156 us
    pallas_call x1, Pallas kernels, gather_weights(): pl.pallas_call(functools.partial(gather_kernel, plan), out_shape=tuple((j...  70.6 us
    unnamed x94, local copies, waits for them, and re-layouts  24 us
    dot_general x5, matrix products, matmul(): return jnp.dot(left, right, preferred_element_type=jnp.float32)  20.2 us
    dot_general x4, matrix products, left_inner(): lax.dot_general(left, right, (((0,), (0,)), ((), ())), preferred_element_...  17.4 us
    dot_general x5, matrix products, right_inner(): lax.dot_general(left, right, (((1,), (1,)), ((), ())), preferred_element_...  13.8 us
    reduce_scatter x1, waiting for transfers between devices, body(): lax.psum_scatter(values_back_all.astype(jnp.bfloat16), 'fsdp', scatter_di...  13 us
    dot_general x4, matrix products, scores_for(): jnp.einsum('bgrd,kgd->grbk', grouped, keys_here, preferred_element_type=j...  11.2 us
  transfers between devices with their start and end apart: 2, of which 1 were waited for; matrix products, arithmetic and copies ran while one was open for 8% of the time, Pallas kernels for 0%

profile of v2, /device:TPU:0, one launch (start us, length us, event | category | flops | bytes accessed | tf_op | source)
XLA Modules:
  0.0 451.2 jit_solution(16635448774772618986)
XLA Ops:
  17.4 70.6 %gather_weights.1 = (bf16[960,2560]{1,0:T(8,128)(2,1)S(1)}, bf16[960,2560]{1,0:T(8,128)(2,1)S(1)}, bf16[960,2560]{1,0:T(8,128)(2,1)S(1)}, bf16[2560,960]{1,0:T(8,128)(2,1)}, bf16[64,256]{1,0:T(8,128)(2,1)S(1)}) custom-call(bf16[240,2560]{1,0:T(8,128)(2,1)S(1)} %concatenate.33.refs_0_, bf16[240,2560]{1,0:T(8,128)(2,1)S(1)} %copy-done.2, ...), custom_call_target="tpu_custom_call" | custom-call | tf_op jit(solution)/shard_map/gather_weights/pallas_call | solution.py:422
  96.1 3.5 fusion.71
  100.6 8.1 %all_gather.6 = bf16[1024,320]{0,1:T(8,128)(2,1)S(1)} all-gather(bf16[256,320]{0,1:T(8,128)(2,1)S(1)} %slice.150), channel_id=1, replica_groups=mesh['rep'=8,'fsdp'=4] {'fsdp'}, dimensions={0}, use_global_device_ids=true | all-gather | bytes 819200 | tf_op jit(solution)/shard_map/all_gather | solution.py:492
  113.1 8.2 %all_gather.7 = bf16[1024,320]{0,1:T(8,128)(2,1)S(1)} all-gather(bf16[256,320]{0,1:T(8,128)(2,1)S(1)} %bitcast.287), channel_id=1, replica_groups=mesh['rep'=8,'fsdp'=4] {'fsdp'}, dimensions={0}, use_global_device_ids=true | all-gather | bytes 819200 | tf_op jit(solution)/shard_map/all_gather | solution.py:491
  122.1 20.9 %while.39 = (s32[]{:T(128)}, f32[5,3,256,1]{2,1,0,3:T(4,128)S(1)}, f32[5,3,256,1]{2,1,0,3:T(4,128)S(1)}, s32[2,512]{1,0:T(2,128)S(1)}, s32[2,512]{1,0:T(2,128)S(...) while((s32[]{:T(128)}, f32[5,3,256,1]{2,1,0,3:T(4,128)S(1)}, ...), condition=%wide.region_7.8_spmd.clone, body=%wide.region_4.7_spmd.clone.sunk | while | flops 267799552 | bytes 17156236 | solution.py:526
  123.0 4.4 fusion.165
  127.4 5.1 %select_reduce_fusion.3 = f32[5,3,256]{2,1,0:T(4,128)S(1)} fusion(f32[5,512,256,3]{2,1,3,0:T(8,128)} %get-tuple-element.791, f32[5,3,256]{2,1,0:T(4,128)S(1)} %bitcast.275, pred[256,512]{0,1:T(8,128)(4,1)S(1)} %compare_and_fusion.6), kind=kLoop, calls=%fused_computation.4.clone.1 | loop fusion | flops 9826560 | bytes 8026112 | tf_op jit(solution)/shard_map/while/body/eval_jaxpr/reduce_sum | solution.py:520
  133.5 4.4 fusion.165
  137.9 5.1 %select_reduce_fusion.3 = f32[5,3,256]{2,1,0:T(4,128)S(1)} fusion(f32[5,512,256,3]{2,1,3,0:T(8,128)} %get-tuple-element.791, f32[5,3,256]{2,1,0:T(4,128)S(1)} %bitcast.275, pred[256,512]{0,1:T(8,128)(4,1)S(1)} %compare_and_fusion.6), kind=kLoop, calls=%fused_computation.4.clone.1 | loop fusion | flops 9826560 | bytes 8026112 | tf_op jit(solution)/shard_map/while/body/eval_jaxpr/reduce_sum | solution.py:520
  143.0 11.7 %while.40 = (s32[]{:T(128)}, f32[256,5,3,64]{0,3,2,1:T(8,128)}, bf16[2,512,5,64]{1,3,2,0:T(8,128)(2,1)}, s32[2,512]{1,0:T(2,128)S(1)}, s32[2,512]{1,0:T(2,128)S(...) while((s32[]{:T(128)}, f32[256,5,3,64]{0,3,2,1:T(8,128)}, ...), condition=%wide.region_9.10_spmd.clone, body=%wide.region_8.9_spmd.clone.sunk | while | flops 514031872 | bytes 3412622 | solution.py:542
  144.0 4.6 %fusion.170 = f32[256,5,3,64]{0,3,2,1:T(8,128)} fusion(f32[5,3,256]{2,1,0:T(4,128)S(1)} %bitcast.301, pred[256,512]{0,1:T(8,128)(4,1)S(1)} %compare_and_fusion.7, bf16[256,5,3,64]{0,3,2,1:T(8,128)(2,1)S(1)} %get-tuple-element.884, f32[256,5,3,64]{0,3,2,1:T(8,128)} %get-tuple-element.866, pred[]{:T(512)S(6)} %compare.56, ...), kind=kOutput, calls=%fused_computation.26.clone.1 | convolution fusion | flops 513638400 | bytes 3266048 | tf_op jit(solution)/shard_map/while/body/eval_jaxpr/grbk,kgd->bgrd/dot_general | solution.py:538
  149.6 5.0 %fusion.170 = f32[256,5,3,64]{0,3,2,1:T(8,128)} fusion(f32[5,3,256]{2,1,0:T(4,128)S(1)} %bitcast.301, pred[256,512]{0,1:T(8,128)(4,1)S(1)} %compare_and_fusion.7, bf16[256,5,3,64]{0,3,2,1:T(8,128)(2,1)S(1)} %get-tuple-element.884, f32[256,5,3,64]{0,3,2,1:T(8,128)} %get-tuple-element.866, pred[]{:T(512)S(6)} %compare.56, ...), kind=kOutput, calls=%fused_computation.26.clone.1 | convolution fusion | flops 513638400 | bytes 3266048 | tf_op jit(solution)/shard_map/while/body/eval_jaxpr/grbk,kgd->bgrd/dot_general | solution.py:538
  156.0 4.7 %multiply_reduce_fusion.3 = (f32[256]{0:T(256)S(1)}, f32[256,960]{0,1:T(8,128)}) fusion(bf16[256,960]{0,1:T(8,128)(2,1)S(1)} %bitcast.282, bf16[960,2560]{1,0:T(8,128)(2,1)} %copy-done.4, bf16[256,960]{0,1:T(8,128)(2,1)S(1)} %copy-done.18), kind=kOutput, calls=%fused_computation.123 | convolution fusion | flops 472841984 | bytes 3933184 | tf_op jit(solution)/shard_map/dot_general | solution.py:41
  162.2 4.1 fusion.114
  167.9 6.3 %multiply_convert_fusion = (bf16[256,2560]{1,0:T(8,128)(2,1)S(1)}, bf16[256,2560]{1,0:T(8,128)(2,1)S(1)}, bf16[256,2560]{1,0:T(8,128)(2,1)}) fusion(f32[256,2560]{1,0:T(8,128)S(1)} %fusion.114, f32[256,2560]{1,0:T(8,128)S(1)} %fusion.115, bf16[2560,960]{1,0:T(8,128)(2,1)} %get-tuple-element.201, bf16[256,960]{0,1:T(8,128)(2,1)S(1)} %copy-done.14), kind=kOutput, calls=%fused_computation.86 | convolution fusion | flops 1268121600 | bytes 14581760 | tf_op jit(solution)/shard_map/dot_general | solution.py:51
  181.6 29.9 %while.41 = (s32[]{:T(128)}, f32[256,5,3,64]{0,3,2,1:T(8,128)S(1)}, bf16[2,512,5,64]{1,3,2,0:T(8,128)(2,1)}, bf16[2,512,5,64]{1,3,2,0:T(8,128)(2,1)}, bf16[2,512...) while((s32[]{:T(128)}, f32[256,5,3,64]{0,3,2,1:T(8,128)S(1)}, ...), condition=%wide.region_14.15_spmd.clone, body=%wide.region_13.14_spmd.clone.sunk | while | flops 1282932992 | bytes 128593264 | solution.py:597
  183.5 4.2 fusion.182
  187.7 3.1 fusion.183
  198.2 4.2 fusion.182
  202.4 3.1 fusion.183
  217.1 3.0 convolution_convert_fusion.3
  220.1 6.4 %fusion.83 = bf16[256,960]{0,1:T(8,128)(2,1)} fusion(f32[256,960]{0,1:T(8,128)} %get-tuple-element.600, bf16[256,2560]{1,0:T(8,128)(2,1)} %get-tuple-element.575, bf16[2560,960]{1,0:T(8,128)(2,1)} %get-tuple-element.201), kind=kOutput, calls=%fused_computation.104 | convolution fusion | flops 1258782720 | bytes 7700480 | tf_op jit(solution)/shard_map/dot_general | solution.py:41
  226.5 3.6 convolution_convert_fusion.1
  231.2 8.1 %copy.91.refs_2_ = bf16[2560,960]{1,0:T(8,128)(2,1)} copy(bf16[2560,960]{0,1:T(8,128)(2,1)} %convolution_convert_fusion.1) | data formatting | bytes 9830400 | tf_op jit(solution)/shard_map/convert_element_type | solution.py:631
  240.3 8.2 %convolution_convert_fusion.refs_1_ = bf16[960,5120]{1,0:T(8,128)(2,1)} fusion(bf16[256,960]{0,1:T(8,128)(2,1)S(1)} %multiply_convert_fusion.3, bf16[256,2560]{1,0:T(8,128)(2,1)} %copy-done.22, bf16[256,2560]{1,0:T(8,128)(2,1)} %copy-done.23), kind=kOutput, calls=%fused_computation.74 | convolution fusion | flops 2526740480 | bytes 12943360 | tf_op jit(solution)/shard_map/dot_general | solution.py:45
  249.6 13.0 %reduce-scatter.5.cloned.1.call-done = bf16[256,320]{0,1:T(8,128)(2,1)} async-done(((bf16[1024,320]{0,1:T(8,128)(2,1)}), bf16[256,320]{0,1:T(8,128)(2,1)}) %reduce-scatter.5.cloned.1.call-update) | async-done | bytes 163856 | tf_op jit(solution)/shard_map/reduce_scatter | solution.py:606
  262.6 2.5 convolution_convert_fusion.2
  265.2 3.5 pad_maximum_fusion.refs_0_
  271.5 155.9 %reduce_grads.1 = (bf16[240,2560]{1,0:T(8,128)(2,1)}, bf16[240,5120]{1,0:T(8,128)(2,1)}, bf16[640,960]{1,0:T(8,128)(2,1)}, f32[8,1024]{1,0:T(8,128)}) custom-call(bf16[960,2560]{1,0:T(8,128)(2,1)} %pad_maximum_fusion.refs_0_, bf16[960,5120]{1,0:T(8,128)(2,1)} %convolution_convert_fusion.refs_1_, bf16[2560,960]{1,0:T(8,128)(2,1)} %copy.91.refs_2_, ...), custom_call_target="tpu_custom_call" | custom-call | tf_op jit(solution)/shard_map/reduce_grads/pallas_call | solution.py:319
  427.4 2.9 slice_convert_fusion.2
  435.9 2.9 slice_convert_fusion
  438.8 2.9 copy.94
  (215 shorter events, 73.9 us)
Async XLA Ops:
  7.2 241.4 %reduce-scatter.3.cloned.1.call-start = ((), (), s32[]{:S(2)}) async-start(), calls=%async_computation.2 | async-start | bytes 819200 | tf_op jit(solution)/shard_map/reduce_scatter | solution.py:603
  11.0 84.3 %copy-start.17 = (bf16[256,960]{0,1:T(8,128)(2,1)S(1)}, bf16[256,960]{0,1:T(8,128)(2,1)}, u32[]{:S(2)}) copy-start(bf16[256,960]{0,1:T(8,128)(2,1)} %param.18) | copy-start | bytes 1474564
  95.4 5.1 %copy-start.34 = (f32[960]{0:T(1024)}, f32[960]{0:T(1024)S(1)}, u32[]{:S(2)}) copy-start(f32[960]{0:T(1024)S(1)} %reshape.405) | copy-start | bytes 11524
  96.1 4.4 copy-start.38
  99.7 10.5 %copy-start.41 = (s32[1,8]{1,0:T(1,128)S(1)}, s32[1,8]{1,0:T(1,128)}, u32[]{:S(2)}) copy-start(s32[1,8]{1,0:T(1,128)} %param.20) | copy-start | bytes 100
  112.0 10.0 %copy-start.26 = (f32[256,32]{0,1:T(8,128)}, f32[256,32]{0,1:T(8,128)S(1)}, u32[]{:S(2)}) copy-start(f32[256,32]{0,1:T(8,128)S(1)} %get-tuple-element.594) | copy-start | bytes 98308
  143.0 13.0 %copy-start.18 = (bf16[256,960]{0,1:T(8,128)(2,1)S(1)}, bf16[256,960]{0,1:T(8,128)(2,1)}, u32[]{:S(2)}) copy-start(bf16[256,960]{0,1:T(8,128)(2,1)} %param.18) | copy-start | bytes 1474564
  154.7 6.0 %copy-start.36 = (f32[4,240]{1,0:T(4,128)S(1)}, f32[4,240]{1,0:T(4,128)}, u32[]{:S(2)}) copy-start(f32[4,240]{1,0:T(4,128)} %get-tuple-element.497) | copy-start | bytes 11524
  156.0 4.7 %copy-start.21 = (bf16[256,5,3,64]{0,3,2,1:T(8,128)(2,1)}, bf16[256,5,3,64]{0,3,2,1:T(8,128)(2,1)S(1)}, u32[]{:S(2)}) copy-start(bf16[256,5,3,64]{0,3,2,1:T(8,128)(2,1)S(1)} %convert_element_type.155) | copy-start | bytes 1474564
  156.0 10.3 %slice-start = ((s8[4915200]{0:T(1024)(128)(4,1)}), s8[720896]{0:T(1024)(128)(4,1)S(1)}, s32[]{:S(2)}) async-start(s8[4915200]{0:T(1024)(128)(4,1)} %bitcast.268), calls=%async_computation.4 | async-start | bytes 1441792
  162.2 4.1 slice-start.1
  166.3 7.9 %slice-start.2 = ((s8[4915200]{0:T(1024)(128)(4,1)}), s8[4194304]{0:T(1024)(128)(4,1)S(1)}, s32[]{:S(2)}) async-start(s8[4915200]{0:T(1024)(128)(4,1)} %bitcast.270), calls=%async_computation.6 | async-start | bytes 8388608
  167.9 6.3 %slice-start.3 = ((s8[4915200]{0:T(1024)(128)(4,1)}), s8[720896]{0:T(1024)(128)(4,1)S(1)}, s32[]{:S(2)}) async-start(s8[4915200]{0:T(1024)(128)(4,1)} %bitcast.270), calls=%async_computation.7 | async-start | bytes 1441792
  177.8 3.7 copy-start.12
  177.8 3.8 copy-start.33
  183.2 4.4 copy-start.6
  187.7 5.6 %copy-start.7 = (f32[5,512,256,3]{2,1,3,0:T(8,128)S(1)}, f32[5,512,256,3]{2,1,3,0:T(8,128)}, u32[]{:S(2)}) copy-start(f32[5,512,256,3]{2,1,3,0:T(8,128)} %copy-done.6) | copy-start | bytes 23592964 | tf_op jit(solution)/shard_map/while
  198.0 4.4 copy-start.6
  202.4 5.6 %copy-start.7 = (f32[5,512,256,3]{2,1,3,0:T(8,128)S(1)}, f32[5,512,256,3]{2,1,3,0:T(8,128)}, u32[]{:S(2)}) copy-start(f32[5,512,256,3]{2,1,3,0:T(8,128)} %copy-done.6) | copy-start | bytes 23592964 | tf_op jit(solution)/shard_map/while
  211.5 5.6 %copy-start.9 = (f32[256,960]{0,1:T(8,128)S(1)}, f32[256,960]{0,1:T(8,128)}, u32[]{:S(2)}) copy-start(f32[256,960]{0,1:T(8,128)} %copy-done.8) | copy-start | bytes 2949124
  214.3 48.3 %reduce-scatter.5.cloned.1.call-start = ((), (), s32[]{:S(2)}) async-start(), calls=%async_computation.3 | async-start | bytes 819200 | tf_op jit(solution)/shard_map/reduce_scatter | solution.py:606
  220.1 6.4 %copy-start.15 = (bf16[256,960]{0,1:T(8,128)(2,1)S(1)}, bf16[256,960]{0,1:T(8,128)(2,1)}, u32[]{:S(2)}) copy-start(bf16[256,960]{0,1:T(8,128)(2,1)} %param.19) | copy-start | bytes 1474564
  220.1 6.4 %copy-start.24 = (bf16[256,2560]{1,0:T(8,128)(2,1)S(1)}, bf16[256,2560]{1,0:T(8,128)(2,1)}, u32[]{:S(2)}) copy-start(bf16[256,2560]{1,0:T(8,128)(2,1)} %get-tuple-element.575) | copy-start | bytes 3932164
  231.2 8.2 %copy-start.13 = (f32[256,5,3,64]{0,3,2,1:T(8,128)S(1)}, f32[256,5,3,64]{0,3,2,1:T(8,128)}, u32[]{:S(2)}) copy-start(f32[256,5,3,64]{0,3,2,1:T(8,128)} %broadcast_multiply_fusion) | copy-start | bytes 2949124
  231.2 8.2 %copy-start.27 = (f32[256,32]{0,1:T(8,128)S(1)}, f32[256,32]{0,1:T(8,128)}, u32[]{:S(2)}) copy-start(f32[256,32]{0,1:T(8,128)} %copy-done.26) | copy-start | bytes 98308
  231.2 8.2 %copy-start.32 = (f32[256,32]{0,1:T(8,128)S(1)}, f32[256,32]{0,1:T(8,128)}, u32[]{:S(2)}) copy-start(f32[256,32]{0,1:T(8,128)} %get-tuple-element.592) | copy-start | bytes 98308
  240.3 22.3 %copy-start.35 = (f32[960]{0:T(1024)S(1)}, f32[960]{0:T(1024)}, u32[]{:S(2)}) copy-start(f32[960]{0:T(1024)} %copy-done.34) | copy-start | bytes 11524
  240.3 22.3 %copy-start.39 = (f32[256]{0:T(256)S(1)}, f32[256]{0:T(256)}, u32[]{:S(2)}) copy-start(f32[256]{0:T(256)} %copy-done.38) | copy-start | bytes 3076
  249.5 15.7 %copy-start.10 = (bf16[960,960]{1,0:T(8,128)(2,1)S(1)}, bf16[960,960]{1,0:T(8,128)(2,1)}, u32[]{:S(2)}) copy-start(bf16[960,960]{1,0:T(8,128)(2,1)} %convolution_convert_fusion.3) | copy-start | bytes 5529604
  262.6 6.1 %slice-start.4 = ((s8[4915200]{0:T(1024)(128)(4,1)}), s8[4194304]{0:T(1024)(128)(4,1)S(1)}, s32[]{:S(2)}) async-start(s8[4915200]{0:T(1024)(128)(4,1)} %bitcast.273), calls=%async_computation.8 | async-start | bytes 8388608
  427.4 8.6 %copy-start.16 = (bf16[240,5120]{1,0:T(8,128)(2,1)S(1)}, bf16[240,5120]{1,0:T(8,128)(2,1)}, u32[]{:S(2)}) copy-start(bf16[240,5120]{1,0:T(8,128)(2,1)} %get-tuple-element.207) | copy-start | bytes 7372804
  435.9 5.8 %copy-start.37 = (f32[256]{0:T(256)S(1)}, f32[256]{0:T(256)}, u32[]{:S(2)}) copy-start(f32[256]{0:T(256)} %get-tuple-element.595) | copy-start | bytes 3076
  (24 other events, 53.8 us)
Sparse Core Ops, SparseCore 0:
  214.4 23.1 reduce-scatter.2
  240.2 22.4 reduce-scatter.4
